TPU v7x, 32 devices: a whole 2x2x4 slice. The times are simulated.
32 devices in a mesh: ka: 16 (over z, y, core), rad: 2 (over x).
Axes of the slice: x: 2, y: 2, z: 4, core: 2. Of those that a mesh axis runs over, the one named last changes fastest.
Arguments:
- prev_wave: float32 [16, 192, 16, 128], P('ka', None, 'rad'), may hold values from -6 to 6
- cur_wave: float32 [16, 192, 16, 128], P('ka', None, 'rad'), may hold values from -6 to 6
- legendre: float32 [16, 192, 192], P('ka'), may hold values from -0.4375 to 0.4375
- potential: float32 [192, 16, 128], P(None, 'rad'), may hold values from -0.15 to 0.15
- radial: float32 [3, 16], P(None, 'rad'), may hold values from 0.02 to 0.3
- rot_const: float32 [128], replicated, may hold values from 0.05 to 0.5
- first_row: int32 [16], P('ka'), may hold values from 0 to 96, as said below
Outputs:
- prev_out: float32 [16, 192, 16, 128], P('ka', None, 'rad')
- cur_out: float32 [16, 192, 16, 128], P('ka', None, 'rad')
Inputs may be any that keep to these rules, and one draw needn't show every extreme that they name: first_row never falls with K, first_row[0] = 0 and first_row[15] = 96.
All inputs are finite; a program needn't handle non-finite values.
Results may differ from a plain program's by a relative error of at most 0.0003.
Values sent between devices are 32-bit elements; how exact they have to be, the bound alone decides.
A program may use at most 64 MiB of HBM per device.

v0:
```python
import math

import jax
import jax.numpy as jnp
from jax import lax
from jax.sharding import PartitionSpec as P

STEPS = 4
KICKS = 2


COEF = 0.1
RKIN = 0.04
EMID = 0.75


def with_halo(array, sides, width):
    for axis, dim in sides:
        size, length = (lax.axis_size(axis), array.shape[dim])
        up = [(i, (i + 1) % size) for i in range(size - 1)]
        down = [(j, i) for i, j in up]
        last = lax.slice_in_dim(array, length - width, length, axis=dim)
        leading = lax.slice_in_dim(array, 0, width, axis=dim)
        before = lax.ppermute(last, axis, up)
        after = lax.ppermute(leading, axis, down)
        array = jnp.concatenate([before, array, after], axis=dim)
    return array


def sinc_table(count):
    index = jnp.arange(count, dtype=jnp.int32)
    differ = index[:, None] - index[None, :]
    parity = (1 - 2 * (jnp.abs(differ) % 2)).astype(jnp.float32)
    square = jnp.maximum(differ * differ, 1).astype(jnp.float32)
    table = jnp.where(differ == 0, jnp.float32(math.pi * math.pi / 3.0), 2.0 * parity / square)
    return RKIN * table


def coupling(jidx, kval, jtop, nrot):
    first = jnp.maximum(jidx * (jidx + 1) - kval * (kval + 1), 0)
    second = jnp.maximum(jtop * (jtop + 1) - kval * (kval + 1), 0)
    return jnp.sqrt((first * second).astype(jnp.float32)) / (nrot * (jtop + 1))


def make_diag(rot_const, qrot, centri, pkay):
    return (
        rot_const[None, None, :] * qrot[:, None, None]
        + centri[None, :, None] * (qrot[:, None, None] + pkay)
        - EMID
    )


def chain_pair(wave):
    chained = with_halo(wave[None], (("ka", 0),), 1)
    lower = chained[0]
    upper = chained[2]
    return (lower, upper)


def apply_h(
    wave,
    below,
    above,
    lower,
    upper,
    transform,
    potent,
    diag,
    live,
    table,
    corio,
    couple_here,
    couple_below,
):
    nrot, rows, width = wave.shape
    stencil = 2.0 * wave - above - below
    kinetic = jnp.dot(
        wave.reshape(nrot * rows, width), table, precision=lax.Precision.HIGHEST
    ).reshape(wave.shape)
    angular = lax.dot_general(
        transform,
        wave.reshape(nrot, rows * width),
        (((0,), (0,)), ((), ())),
        precision=lax.Precision.HIGHEST,
    )
    back = jnp.dot(
        transform, potent.reshape(nrot, rows * width) * angular, precision=lax.Precision.HIGHEST
    ).reshape(wave.shape)
    coriolis = corio * (couple_here * upper + couple_below * lower)
    return live * (COEF * stencil + kinetic + diag * wave + back + coriolis)


def on_device(prev_wave, cur_wave, legendre, potential, radial, rot_const, first_row):
    kpos = lax.axis_index("ka")
    jtop = lax.axis_size("ka") - 1
    nrot = cur_wave.shape[1]
    width = cur_wave.shape[3]
    jidx = jnp.arange(nrot, dtype=jnp.int32)
    live = (jidx >= first_row[0]).astype(jnp.float32)[:, None, None]
    qrot = (jidx * (jidx + 1)).astype(jnp.float32) / (nrot * (nrot + 1))
    pkay = (jtop * (jtop + 1) - 2 * kpos * kpos).astype(jnp.float32) / (nrot * (nrot + 1))
    couple_here = coupling(jidx, kpos, jtop, nrot)[:, None, None]
    couple_below = coupling(jidx, kpos - 1, jtop, nrot)[:, None, None]
    table = sinc_table(width)
    transform = legendre[0]
    prev = live * prev_wave[0]
    cur = live * cur_wave[0]
    damp = jnp.exp(-radial[2])[None, :, None]
    corio = radial[1][None, :, None]
    diag = make_diag(rot_const, qrot, radial[0], pkay)
    for kick_turn in range(KICKS):
        for step in range(STEPS):
            lower, upper = chain_pair(cur)
            rimmed = with_halo(cur, (("rad", 1),), 1)
            applied = apply_h(
                cur,
                rimmed[:, :-2],
                rimmed[:, 2:],
                lower,
                upper,
                transform,
                potential,
                diag,
                live,
                table,
                corio,
                couple_here,
                couple_below,
            )
            newer = damp * (2.0 * applied - damp * prev)
            prev, cur = (cur, newer)
    return (prev[None], cur[None])


def solution(mesh):
    placed = (
        P("ka", None, "rad", None),
        P("ka", None, "rad", None),
        P("ka", None, None),
        P(None, "rad", None),
        P(None, "rad"),
        P(),
        P("ka"),
    )
    return jax.shard_map(
        on_device,
        mesh=mesh,
        in_specs=placed,
        out_specs=(P("ka", None, "rad", None), P("ka", None, "rad", None)),
        check_vma=False,
    )
```

profile of v0, /device:TPU:1, one launch (start us, length us, event | category | flops | bytes accessed | tf_op | source)
XLA Modules:
  0.0 184.9 jit_solution(2079921706238704341)
XLA Ops:
  2.8 4.7 %collective-permute-start.3 = (f32[1,192,8,128]{3,2,1,0:T(8,128)S(1)}, f32[1,192,8,128]{3,2,1,0:T(8,128)}, u32[]{:S(2)}, u32[]{:S(2)}) collective-permute-start(f32[1,192,8,128]{3,2,1,0:T(8,128)S(1)} %broadcast_multiply_fusion), channel_id=1, source_target_pairs={{0,2},{2,4},{4,6},{6,8},{8,10},{10,12},{12,14},{14,16},{16,18},{18... | collective-permute-start | bytes 2359304 | tf_op jit(solution)/shard_map/ppermute | solution.py:24
  11.2 5.2 %collective-permute-start.1 = (f32[192,1,128]{2,1,0:T(1,128)S(1)}, f32[192,1,128]{2,1,0:T(1,128)}, u32[]{:S(2)}, u32[]{:S(2)}) collective-permute-start(f32[192,1,128]{2,1,0:T(1,128)S(1)} %get-tuple-element.17), channel_id=1, source_target_pairs={{0,1},{2,3},{4,5},{6,7},{8,9},{10,11},{12,13},{14,15},{16,17},{18,... | collective-permute-start | bytes 294920 | tf_op jit(solution)/shard_map/ppermute | solution.py:24
  19.9 5.0 %collective-permute-done.3 = f32[1,192,8,128]{3,2,1,0:T(8,128)} collective-permute-done((f32[1,192,8,128]{3,2,1,0:T(8,128)S(1)}, f32[1,192,8,128]{3,2,1,0:T(8,128)}, u32[]{:S(2)}, u32[]{:S(2)}) %collective-permute-start.3) | collective-permute-done | bytes 786464 | tf_op jit(solution)/shard_map/ppermute | solution.py:24
  28.3 4.5 %collective-permute-start.7 = (f32[1,192,8,128]{3,2,1,0:T(8,128)S(1)}, f32[1,192,8,128]{3,2,1,0:T(8,128)S(1)}, u32[]{:S(2)}, u32[]{:S(2)}) collective-permute-start(f32[1,192,8,128]{3,2,1,0:T(8,128)S(1)} %bitcast.411), channel_id=1, source_target_pairs={{0,2},{2,4},{4,6},{6,8},{8,10},{10,12},{12,14},{14,16},{16,18},{18... | collective-permute-start | bytes 2359304 | tf_op jit(solution)/shard_map/ppermute | solution.py:24
  36.2 4.0 %collective-permute-start.5 = (f32[192,1,128]{2,1,0:T(1,128)S(1)}, f32[192,1,128]{2,1,0:T(1,128)S(1)}, u32[]{:S(2)}, u32[]{:S(2)}) collective-permute-start(f32[192,1,128]{2,1,0:T(1,128)S(1)} %get-tuple-element.15), channel_id=1, source_target_pairs={{0,1},{2,3},{4,5},{6,7},{8,9},{10,11},{12,13},{14,15},{16,17},{18,... | collective-permute-start | bytes 294920 | tf_op jit(solution)/shard_map/ppermute | solution.py:24
  43.1 7.0 %collective-permute-done.7 = f32[1,192,8,128]{3,2,1,0:T(8,128)S(1)} collective-permute-done((f32[1,192,8,128]{3,2,1,0:T(8,128)S(1)}, f32[1,192,8,128]{3,2,1,0:T(8,128)S(1)}, u32[]{:S(2)}, u32[]{:S(2)}) %collective-permute-start.7) | collective-permute-done | bytes 786464 | tf_op jit(solution)/shard_map/ppermute | solution.py:24
  51.4 4.4 %collective-permute-start.11 = (f32[1,192,8,128]{3,2,1,0:T(8,128)S(1)}, f32[1,192,8,128]{3,2,1,0:T(8,128)S(1)}, u32[]{:S(2)}, u32[]{:S(2)}) collective-permute-start(f32[1,192,8,128]{3,2,1,0:T(8,128)S(1)} %bitcast.414), channel_id=1, source_target_pairs={{0,2},{2,4},{4,6},{6,8},{8,10},{10,12},{12,14},{14,16},{16,18},{18... | collective-permute-start | bytes 2359304 | tf_op jit(solution)/shard_map/ppermute | solution.py:24
  59.2 4.0 %collective-permute-start.9 = (f32[192,1,128]{2,1,0:T(1,128)S(1)}, f32[192,1,128]{2,1,0:T(1,128)S(1)}, u32[]{:S(2)}, u32[]{:S(2)}) collective-permute-start(f32[192,1,128]{2,1,0:T(1,128)S(1)} %get-tuple-element.13), channel_id=1, source_target_pairs={{0,1},{2,3},{4,5},{6,7},{8,9},{10,11},{12,13},{14,15},{16,17},{18,... | collective-permute-start | bytes 294920 | tf_op jit(solution)/shard_map/ppermute | solution.py:24
  65.3 7.9 %collective-permute-done.11 = f32[1,192,8,128]{3,2,1,0:T(8,128)S(1)} collective-permute-done((f32[1,192,8,128]{3,2,1,0:T(8,128)S(1)}, f32[1,192,8,128]{3,2,1,0:T(8,128)S(1)}, u32[]{:S(2)}, u32[]{:S(2)}) %collective-permute-start.11) | collective-permute-done | bytes 786464 | tf_op jit(solution)/shard_map/ppermute | solution.py:24
  74.8 4.6 %collective-permute-start.15 = (f32[1,192,8,128]{3,2,1,0:T(8,128)S(1)}, f32[1,192,8,128]{3,2,1,0:T(8,128)S(1)}, u32[]{:S(2)}, u32[]{:S(2)}) collective-permute-start(f32[1,192,8,128]{3,2,1,0:T(8,128)S(1)} %bitcast.402), channel_id=1, source_target_pairs={{0,2},{2,4},{4,6},{6,8},{8,10},{10,12},{12,14},{14,16},{16,18},{18... | collective-permute-start | bytes 2359304 | tf_op jit(solution)/shard_map/ppermute | solution.py:24
  82.8 4.0 %collective-permute-start.13 = (f32[192,1,128]{2,1,0:T(1,128)S(1)}, f32[192,1,128]{2,1,0:T(1,128)S(1)}, u32[]{:S(2)}, u32[]{:S(2)}) collective-permute-start(f32[192,1,128]{2,1,0:T(1,128)S(1)} %get-tuple-element.11), channel_id=1, source_target_pairs={{0,1},{2,3},{4,5},{6,7},{8,9},{10,11},{12,13},{14,15},{16,17},{18,... | collective-permute-start | bytes 294920 | tf_op jit(solution)/shard_map/ppermute | solution.py:24
  89.7 6.8 %collective-permute-done.15 = f32[1,192,8,128]{3,2,1,0:T(8,128)S(1)} collective-permute-done((f32[1,192,8,128]{3,2,1,0:T(8,128)S(1)}, f32[1,192,8,128]{3,2,1,0:T(8,128)S(1)}, u32[]{:S(2)}, u32[]{:S(2)}) %collective-permute-start.15) | collective-permute-done | bytes 786464 | tf_op jit(solution)/shard_map/ppermute | solution.py:24
  97.8 4.4 %collective-permute-start.19 = (f32[1,192,8,128]{3,2,1,0:T(8,128)S(1)}, f32[1,192,8,128]{3,2,1,0:T(8,128)S(1)}, u32[]{:S(2)}, u32[]{:S(2)}) collective-permute-start(f32[1,192,8,128]{3,2,1,0:T(8,128)S(1)} %bitcast.405), channel_id=1, source_target_pairs={{0,2},{2,4},{4,6},{6,8},{8,10},{10,12},{12,14},{14,16},{16,18},{18... | collective-permute-start | bytes 2359304 | tf_op jit(solution)/shard_map/ppermute | solution.py:24
  105.6 4.0 %collective-permute-start.17 = (f32[192,1,128]{2,1,0:T(1,128)S(1)}, f32[192,1,128]{2,1,0:T(1,128)S(1)}, u32[]{:S(2)}, u32[]{:S(2)}) collective-permute-start(f32[192,1,128]{2,1,0:T(1,128)S(1)} %get-tuple-element.9), channel_id=1, source_target_pairs={{0,1},{2,3},{4,5},{6,7},{8,9},{10,11},{12,13},{14,15},{16,17},{18,... | collective-permute-start | bytes 294920 | tf_op jit(solution)/shard_map/ppermute | solution.py:24
  111.7 7.9 %collective-permute-done.19 = f32[1,192,8,128]{3,2,1,0:T(8,128)S(1)} collective-permute-done((f32[1,192,8,128]{3,2,1,0:T(8,128)S(1)}, f32[1,192,8,128]{3,2,1,0:T(8,128)S(1)}, u32[]{:S(2)}, u32[]{:S(2)}) %collective-permute-start.19) | collective-permute-done | bytes 786464 | tf_op jit(solution)/shard_map/ppermute | solution.py:24
  121.2 4.4 %collective-permute-start.23 = (f32[1,192,8,128]{3,2,1,0:T(8,128)S(1)}, f32[1,192,8,128]{3,2,1,0:T(8,128)S(1)}, u32[]{:S(2)}, u32[]{:S(2)}) collective-permute-start(f32[1,192,8,128]{3,2,1,0:T(8,128)S(1)} %bitcast.408), channel_id=1, source_target_pairs={{0,2},{2,4},{4,6},{6,8},{8,10},{10,12},{12,14},{14,16},{16,18},{18... | collective-permute-start | bytes 2359304 | tf_op jit(solution)/shard_map/ppermute | solution.py:24
  129.0 4.0 %collective-permute-start.21 = (f32[192,1,128]{2,1,0:T(1,128)S(1)}, f32[192,1,128]{2,1,0:T(1,128)S(1)}, u32[]{:S(2)}, u32[]{:S(2)}) collective-permute-start(f32[192,1,128]{2,1,0:T(1,128)S(1)} %get-tuple-element.7), channel_id=1, source_target_pairs={{0,1},{2,3},{4,5},{6,7},{8,9},{10,11},{12,13},{14,15},{16,17},{18,... | collective-permute-start | bytes 294920 | tf_op jit(solution)/shard_map/ppermute | solution.py:24
  136.0 4.8 %collective-permute-done.23 = f32[1,192,8,128]{3,2,1,0:T(8,128)S(1)} collective-permute-done((f32[1,192,8,128]{3,2,1,0:T(8,128)S(1)}, f32[1,192,8,128]{3,2,1,0:T(8,128)S(1)}, u32[]{:S(2)}, u32[]{:S(2)}) %collective-permute-start.23) | collective-permute-done | bytes 786464 | tf_op jit(solution)/shard_map/ppermute | solution.py:24
  142.0 4.6 %collective-permute-start.27 = (f32[1,192,8,128]{3,2,1,0:T(8,128)S(1)}, f32[1,192,8,128]{3,2,1,0:T(8,128)S(1)}, u32[]{:S(2)}, u32[]{:S(2)}) collective-permute-start(f32[1,192,8,128]{3,2,1,0:T(8,128)S(1)} %bitcast.399), channel_id=1, source_target_pairs={{0,2},{2,4},{4,6},{6,8},{8,10},{10,12},{12,14},{14,16},{16,18},{18... | collective-permute-start | bytes 2359304 | tf_op jit(solution)/shard_map/ppermute | solution.py:24
  150.0 4.0 %collective-permute-start.25 = (f32[192,1,128]{2,1,0:T(1,128)S(1)}, f32[192,1,128]{2,1,0:T(1,128)S(1)}, u32[]{:S(2)}, u32[]{:S(2)}) collective-permute-start(f32[192,1,128]{2,1,0:T(1,128)S(1)} %get-tuple-element.5), channel_id=1, source_target_pairs={{0,1},{2,3},{4,5},{6,7},{8,9},{10,11},{12,13},{14,15},{16,17},{18,... | collective-permute-start | bytes 294920 | tf_op jit(solution)/shard_map/ppermute | solution.py:24
  156.1 5.0 %collective-permute-done.27 = f32[1,192,8,128]{3,2,1,0:T(8,128)S(1)} collective-permute-done((f32[1,192,8,128]{3,2,1,0:T(8,128)S(1)}, f32[1,192,8,128]{3,2,1,0:T(8,128)S(1)}, u32[]{:S(2)}, u32[]{:S(2)}) %collective-permute-start.27) | collective-permute-done | bytes 786464 | tf_op jit(solution)/shard_map/ppermute | solution.py:24
  162.8 4.4 %collective-permute-start.31 = (f32[1,192,8,128]{3,2,1,0:T(8,128)S(1)}, f32[1,192,8,128]{3,2,1,0:T(8,128)S(1)}, u32[]{:S(2)}, u32[]{:S(2)}) collective-permute-start(f32[1,192,8,128]{3,2,1,0:T(8,128)S(1)} %bitcast.417), channel_id=1, source_target_pairs={{0,2},{2,4},{4,6},{6,8},{8,10},{10,12},{12,14},{14,16},{16,18},{18... | collective-permute-start | bytes 2359304 | tf_op jit(solution)/shard_map/ppermute | solution.py:24
  170.6 4.0 %collective-permute-start.29 = (f32[192,1,128]{2,1,0:T(1,128)S(1)}, f32[192,1,128]{2,1,0:T(1,128)S(1)}, u32[]{:S(2)}, u32[]{:S(2)}) collective-permute-start(f32[192,1,128]{2,1,0:T(1,128)S(1)} %get-tuple-element.3), channel_id=1, source_target_pairs={{0,1},{2,3},{4,5},{6,7},{8,9},{10,11},{12,13},{14,15},{16,17},{18,... | collective-permute-start | bytes 294920 | tf_op jit(solution)/shard_map/ppermute | solution.py:24
  177.6 5.1 %collective-permute-done.31 = f32[1,192,8,128]{3,2,1,0:T(8,128)S(1)} collective-permute-done((f32[1,192,8,128]{3,2,1,0:T(8,128)S(1)}, f32[1,192,8,128]{3,2,1,0:T(8,128)S(1)}, u32[]{:S(2)}, u32[]{:S(2)}) %collective-permute-start.31) | collective-permute-done | bytes 786464 | tf_op jit(solution)/shard_map/ppermute | solution.py:24
  (107 shorter events, 64.2 us)
Async XLA Ops:
  2.8 22.0 %collective-permute-start.3 = (f32[1,192,8,128]{3,2,1,0:T(8,128)S(1)}, f32[1,192,8,128]{3,2,1,0:T(8,128)}, u32[]{:S(2)}, u32[]{:S(2)}) collective-permute-start(f32[1,192,8,128]{3,2,1,0:T(8,128)S(1)} %broadcast_multiply_fusion), channel_id=1, source_target_pairs={{0,2},{2,4},{4,6},{6,8},{8,10},{10,12},{12,14},{14,16},{16,18},{18... | collective-permute-start | bytes 2359304 | tf_op jit(solution)/shard_map/ppermute | solution.py:24
  7.5 17.3 %collective-permute-start.2 = (f32[1,192,8,128]{3,2,1,0:T(8,128)S(1)}, f32[1,192,8,128]{3,2,1,0:T(8,128)}, u32[]{:S(2)}, u32[]{:S(2)}) collective-permute-start(f32[1,192,8,128]{3,2,1,0:T(8,128)S(1)} %broadcast_multiply_fusion), channel_id=1, source_target_pairs={{2,0},{4,2},{6,4},{8,6},{10,8},{12,10},{14,12},{16,14},{18,16},{20... | collective-permute-start | bytes 2359304 | tf_op jit(solution)/shard_map/ppermute | solution.py:25
  9.9 10.0 %collective-permute-start = (f32[192,1,128]{2,1,0:T(1,128)S(1)}, f32[192,1,128]{2,1,0:T(1,128)}, u32[]{:S(2)}, u32[]{:S(2)}) collective-permute-start(f32[192,1,128]{2,1,0:T(1,128)S(1)} %get-tuple-element.16), channel_id=1, source_target_pairs={{1,0},{3,2},{5,4},{7,6},{9,8},{11,10},{13,12},{15,14},{17,16},{19,... | collective-permute-start | bytes 294920 | tf_op jit(solution)/shard_map/ppermute | solution.py:25
  11.2 8.7 %collective-permute-start.1 = (f32[192,1,128]{2,1,0:T(1,128)S(1)}, f32[192,1,128]{2,1,0:T(1,128)}, u32[]{:S(2)}, u32[]{:S(2)}) collective-permute-start(f32[192,1,128]{2,1,0:T(1,128)S(1)} %get-tuple-element.17), channel_id=1, source_target_pairs={{0,1},{2,3},{4,5},{6,7},{8,9},{10,11},{12,13},{14,15},{16,17},{18,... | collective-permute-start | bytes 294920 | tf_op jit(solution)/shard_map/ppermute | solution.py:24
  28.3 21.8 %collective-permute-start.7 = (f32[1,192,8,128]{3,2,1,0:T(8,128)S(1)}, f32[1,192,8,128]{3,2,1,0:T(8,128)S(1)}, u32[]{:S(2)}, u32[]{:S(2)}) collective-permute-start(f32[1,192,8,128]{3,2,1,0:T(8,128)S(1)} %bitcast.411), channel_id=1, source_target_pairs={{0,2},{2,4},{4,6},{6,8},{8,10},{10,12},{12,14},{14,16},{16,18},{18... | collective-permute-start | bytes 2359304 | tf_op jit(solution)/shard_map/ppermute | solution.py:24
  32.8 17.3 %collective-permute-start.6 = (f32[1,192,8,128]{3,2,1,0:T(8,128)S(1)}, f32[1,192,8,128]{3,2,1,0:T(8,128)S(1)}, u32[]{:S(2)}, u32[]{:S(2)}) collective-permute-start(f32[1,192,8,128]{3,2,1,0:T(8,128)S(1)} %bitcast.412), channel_id=1, source_target_pairs={{2,0},{4,2},{6,4},{8,6},{10,8},{12,10},{14,12},{16,14},{18,16},{20... | collective-permute-start | bytes 2359304 | tf_op jit(solution)/shard_map/ppermute | solution.py:25
  34.9 8.3 %collective-permute-start.4 = (f32[192,1,128]{2,1,0:T(1,128)S(1)}, f32[192,1,128]{2,1,0:T(1,128)S(1)}, u32[]{:S(2)}, u32[]{:S(2)}) collective-permute-start(f32[192,1,128]{2,1,0:T(1,128)S(1)} %get-tuple-element.14), channel_id=1, source_target_pairs={{1,0},{3,2},{5,4},{7,6},{9,8},{11,10},{13,12},{15,14},{17,16},{19,... | collective-permute-start | bytes 294920 | tf_op jit(solution)/shard_map/ppermute | solution.py:25
  51.4 21.7 %collective-permute-start.11 = (f32[1,192,8,128]{3,2,1,0:T(8,128)S(1)}, f32[1,192,8,128]{3,2,1,0:T(8,128)S(1)}, u32[]{:S(2)}, u32[]{:S(2)}) collective-permute-start(f32[1,192,8,128]{3,2,1,0:T(8,128)S(1)} %bitcast.414), channel_id=1, source_target_pairs={{0,2},{2,4},{4,6},{6,8},{8,10},{10,12},{12,14},{14,16},{16,18},{18... | collective-permute-start | bytes 2359304 | tf_op jit(solution)/shard_map/ppermute | solution.py:24
  55.8 17.3 %collective-permute-start.10 = (f32[1,192,8,128]{3,2,1,0:T(8,128)S(1)}, f32[1,192,8,128]{3,2,1,0:T(8,128)S(1)}, u32[]{:S(2)}, u32[]{:S(2)}) collective-permute-start(f32[1,192,8,128]{3,2,1,0:T(8,128)S(1)} %bitcast.415), channel_id=1, source_target_pairs={{2,0},{4,2},{6,4},{8,6},{10,8},{12,10},{14,12},{16,14},{18,16},{20... | collective-permute-start | bytes 2359304 | tf_op jit(solution)/shard_map/ppermute | solution.py:25
  57.9 7.4 %collective-permute-start.8 = (f32[192,1,128]{2,1,0:T(1,128)S(1)}, f32[192,1,128]{2,1,0:T(1,128)S(1)}, u32[]{:S(2)}, u32[]{:S(2)}) collective-permute-start(f32[192,1,128]{2,1,0:T(1,128)S(1)} %get-tuple-element.12), channel_id=1, source_target_pairs={{1,0},{3,2},{5,4},{7,6},{9,8},{11,10},{13,12},{15,14},{17,16},{19,... | collective-permute-start | bytes 294920 | tf_op jit(solution)/shard_map/ppermute | solution.py:25
  74.8 21.7 %collective-permute-start.15 = (f32[1,192,8,128]{3,2,1,0:T(8,128)S(1)}, f32[1,192,8,128]{3,2,1,0:T(8,128)S(1)}, u32[]{:S(2)}, u32[]{:S(2)}) collective-permute-start(f32[1,192,8,128]{3,2,1,0:T(8,128)S(1)} %bitcast.402), channel_id=1, source_target_pairs={{0,2},{2,4},{4,6},{6,8},{8,10},{10,12},{12,14},{14,16},{16,18},{18... | collective-permute-start | bytes 2359304 | tf_op jit(solution)/shard_map/ppermute | solution.py:24
  79.4 17.2 %collective-permute-start.14 = (f32[1,192,8,128]{3,2,1,0:T(8,128)S(1)}, f32[1,192,8,128]{3,2,1,0:T(8,128)S(1)}, u32[]{:S(2)}, u32[]{:S(2)}) collective-permute-start(f32[1,192,8,128]{3,2,1,0:T(8,128)S(1)} %bitcast.403), channel_id=1, source_target_pairs={{2,0},{4,2},{6,4},{8,6},{10,8},{12,10},{14,12},{16,14},{18,16},{20... | collective-permute-start | bytes 2359304 | tf_op jit(solution)/shard_map/ppermute | solution.py:25
  81.5 8.3 %collective-permute-start.12 = (f32[192,1,128]{2,1,0:T(1,128)S(1)}, f32[192,1,128]{2,1,0:T(1,128)S(1)}, u32[]{:S(2)}, u32[]{:S(2)}) collective-permute-start(f32[192,1,128]{2,1,0:T(1,128)S(1)} %get-tuple-element.10), channel_id=1, source_target_pairs={{1,0},{3,2},{5,4},{7,6},{9,8},{11,10},{13,12},{15,14},{17,16},{19,... | collective-permute-start | bytes 294920 | tf_op jit(solution)/shard_map/ppermute | solution.py:25
  97.8 21.7 %collective-permute-start.19 = (f32[1,192,8,128]{3,2,1,0:T(8,128)S(1)}, f32[1,192,8,128]{3,2,1,0:T(8,128)S(1)}, u32[]{:S(2)}, u32[]{:S(2)}) collective-permute-start(f32[1,192,8,128]{3,2,1,0:T(8,128)S(1)} %bitcast.405), channel_id=1, source_target_pairs={{0,2},{2,4},{4,6},{6,8},{8,10},{10,12},{12,14},{14,16},{16,18},{18... | collective-permute-start | bytes 2359304 | tf_op jit(solution)/shard_map/ppermute | solution.py:24
  102.2 17.3 %collective-permute-start.18 = (f32[1,192,8,128]{3,2,1,0:T(8,128)S(1)}, f32[1,192,8,128]{3,2,1,0:T(8,128)S(1)}, u32[]{:S(2)}, u32[]{:S(2)}) collective-permute-start(f32[1,192,8,128]{3,2,1,0:T(8,128)S(1)} %bitcast.406), channel_id=1, source_target_pairs={{2,0},{4,2},{6,4},{8,6},{10,8},{12,10},{14,12},{16,14},{18,16},{20... | collective-permute-start | bytes 2359304 | tf_op jit(solution)/shard_map/ppermute | solution.py:25
  104.3 7.4 %collective-permute-start.16 = (f32[192,1,128]{2,1,0:T(1,128)S(1)}, f32[192,1,128]{2,1,0:T(1,128)S(1)}, u32[]{:S(2)}, u32[]{:S(2)}) collective-permute-start(f32[192,1,128]{2,1,0:T(1,128)S(1)} %get-tuple-element.8), channel_id=1, source_target_pairs={{1,0},{3,2},{5,4},{7,6},{9,8},{11,10},{13,12},{15,14},{17,16},{19,... | collective-permute-start | bytes 294920 | tf_op jit(solution)/shard_map/ppermute | solution.py:25
  121.2 19.5 %collective-permute-start.23 = (f32[1,192,8,128]{3,2,1,0:T(8,128)S(1)}, f32[1,192,8,128]{3,2,1,0:T(8,128)S(1)}, u32[]{:S(2)}, u32[]{:S(2)}) collective-permute-start(f32[1,192,8,128]{3,2,1,0:T(8,128)S(1)} %bitcast.408), channel_id=1, source_target_pairs={{0,2},{2,4},{4,6},{6,8},{8,10},{10,12},{12,14},{14,16},{16,18},{18... | collective-permute-start | bytes 2359304 | tf_op jit(solution)/shard_map/ppermute | solution.py:24
  125.6 15.1 %collective-permute-start.22 = (f32[1,192,8,128]{3,2,1,0:T(8,128)S(1)}, f32[1,192,8,128]{3,2,1,0:T(8,128)S(1)}, u32[]{:S(2)}, u32[]{:S(2)}) collective-permute-start(f32[1,192,8,128]{3,2,1,0:T(8,128)S(1)} %bitcast.409), channel_id=1, source_target_pairs={{2,0},{4,2},{6,4},{8,6},{10,8},{12,10},{14,12},{16,14},{18,16},{20... | collective-permute-start | bytes 2359304 | tf_op jit(solution)/shard_map/ppermute | solution.py:25
  127.7 8.3 %collective-permute-start.20 = (f32[192,1,128]{2,1,0:T(1,128)S(1)}, f32[192,1,128]{2,1,0:T(1,128)S(1)}, u32[]{:S(2)}, u32[]{:S(2)}) collective-permute-start(f32[192,1,128]{2,1,0:T(1,128)S(1)} %get-tuple-element.6), channel_id=1, source_target_pairs={{1,0},{3,2},{5,4},{7,6},{9,8},{11,10},{13,12},{15,14},{17,16},{19,... | collective-permute-start | bytes 294920 | tf_op jit(solution)/shard_map/ppermute | solution.py:25
  142.0 19.1 %collective-permute-start.27 = (f32[1,192,8,128]{3,2,1,0:T(8,128)S(1)}, f32[1,192,8,128]{3,2,1,0:T(8,128)S(1)}, u32[]{:S(2)}, u32[]{:S(2)}) collective-permute-start(f32[1,192,8,128]{3,2,1,0:T(8,128)S(1)} %bitcast.399), channel_id=1, source_target_pairs={{0,2},{2,4},{4,6},{6,8},{8,10},{10,12},{12,14},{14,16},{16,18},{18... | collective-permute-start | bytes 2359304 | tf_op jit(solution)/shard_map/ppermute | solution.py:24
  146.7 14.5 %collective-permute-start.26 = (f32[1,192,8,128]{3,2,1,0:T(8,128)S(1)}, f32[1,192,8,128]{3,2,1,0:T(8,128)S(1)}, u32[]{:S(2)}, u32[]{:S(2)}) collective-permute-start(f32[1,192,8,128]{3,2,1,0:T(8,128)S(1)} %bitcast.400), channel_id=1, source_target_pairs={{2,0},{4,2},{6,4},{8,6},{10,8},{12,10},{14,12},{16,14},{18,16},{20... | collective-permute-start | bytes 2359304 | tf_op jit(solution)/shard_map/ppermute | solution.py:25
  162.8 19.8 %collective-permute-start.31 = (f32[1,192,8,128]{3,2,1,0:T(8,128)S(1)}, f32[1,192,8,128]{3,2,1,0:T(8,128)S(1)}, u32[]{:S(2)}, u32[]{:S(2)}) collective-permute-start(f32[1,192,8,128]{3,2,1,0:T(8,128)S(1)} %bitcast.417), channel_id=1, source_target_pairs={{0,2},{2,4},{4,6},{6,8},{8,10},{10,12},{12,14},{14,16},{16,18},{18... | collective-permute-start | bytes 2359304 | tf_op jit(solution)/shard_map/ppermute | solution.py:24
  167.2 15.4 %collective-permute-start.30 = (f32[1,192,8,128]{3,2,1,0:T(8,128)S(1)}, f32[1,192,8,128]{3,2,1,0:T(8,128)S(1)}, u32[]{:S(2)}, u32[]{:S(2)}) collective-permute-start(f32[1,192,8,128]{3,2,1,0:T(8,128)S(1)} %bitcast.418), channel_id=1, source_target_pairs={{2,0},{4,2},{6,4},{8,6},{10,8},{12,10},{14,12},{16,14},{18,16},{20... | collective-permute-start | bytes 2359304 | tf_op jit(solution)/shard_map/ppermute | solution.py:25
  169.3 8.3 %collective-permute-start.28 = (f32[192,1,128]{2,1,0:T(1,128)S(1)}, f32[192,1,128]{2,1,0:T(1,128)S(1)}, u32[]{:S(2)}, u32[]{:S(2)}) collective-permute-start(f32[192,1,128]{2,1,0:T(1,128)S(1)} %get-tuple-element.2), channel_id=1, source_target_pairs={{1,0},{3,2},{5,4},{7,6},{9,8},{11,10},{13,12},{15,14},{17,16},{19,... | collective-permute-start | bytes 294920 | tf_op jit(solution)/shard_map/ppermute | solution.py:25
  (15 other events, 118.8 us)
where the time goes:
time: 186 us; the launch traced here: 185 us
  starting transfers between devices  94.8 us (51%)
  waiting for transfers between devices  49.5 us (27%)
  matrix products  27.2 us (15%)
  other arithmetic  8.01 us (4%)
  local copies, waits for them, and re-layouts  3.24 us (2%)
  between operations  2.15 us (1%)
    ppermute x16, starting transfers between devices, with_halo(): before = lax.ppermute(last, axis, up)  69.1 us
    ppermute x16, waiting for transfers between devices, with_halo(): before = lax.ppermute(last, axis, up)  49.4 us
    ppermute x16, starting transfers between devices, with_halo(): after = lax.ppermute(leading, axis, down)  25.7 us
    dot_general x8, matrix products, apply_h(): jnp.dot(wave.reshape(nrot * rows, width), table, precision=lax.Precision....  11.7 us
    dot_general x8, matrix products, apply_h(): lax.dot_general(transform, wave.reshape(nrot, rows * width), (((0,), (0,)...  8.76 us
    dot_general x8, matrix products, apply_h(): jnp.dot(transform, potent.reshape(nrot, rows * width) * angular, precisio...  6.78 us
    mul x4, other arithmetic, on_device(): newer = damp * (2.0 * applied - damp * prev)  6.06 us
  transfers between devices with their start and end apart: 32, of which 8 were waited for; matrix products, arithmetic and copies ran while one was open for 12% of the time, Pallas kernels for 0%

commit v1 on v0

v1 whole, which is shorter than its diff:
```python
import functools
import math

import jax
import jax.numpy as jnp
from jax import lax
from jax.experimental import pallas as pl
from jax.experimental.pallas import tpu as pltpu
from jax.sharding import PartitionSpec as P

STEPS = 4
KICKS = 2
COEF = 0.1
RKIN = 0.04
EMID = 0.75
MESH = pl.DeviceIdType.MESH


def sinc_table(count):
    index = jnp.arange(count, dtype=jnp.int32)
    differ = index[:, None] - index[None, :]
    parity = (1 - 2 * (jnp.abs(differ) % 2)).astype(jnp.float32)
    square = jnp.maximum(differ * differ, 1).astype(jnp.float32)
    table = jnp.where(differ == 0, jnp.float32(math.pi * math.pi / 3.0), 2.0 * parity / square)
    return RKIN * table


def coupling(jidx, kval, jtop, nrot):
    first = jnp.maximum(jidx * (jidx + 1) - kval * (kval + 1), 0)
    second = jnp.maximum(jtop * (jtop + 1) - kval * (kval + 1), 0)
    return jnp.sqrt((first * second).astype(jnp.float32)) / (nrot * (jtop + 1))


def halves(x):
    top = lax.reduce_precision(x, 8, 7)
    return top.astype(jnp.bfloat16), (x - top).astype(jnp.bfloat16)


def split(x):
    top = x.astype(jnp.bfloat16)
    return top, (x - top.astype(jnp.float32)).astype(jnp.bfloat16)


def kernel(
    nka, nrad, steps, rc,
    cur_ref, prev_ref, la_ref, lb_ref, table_ref, pot_ref, diag_ref, shi_ref, slo_ref, scal_ref,
    wave,
    from_lo, from_hi, from_prev, from_next,
    k_send, k_recv, r_send, r_recv,
):
    ka, rad = lax.axis_index("ka"), lax.axis_index("rad")
    m = ka % 4
    y, c = m // 2, m % 2
    pair = (ka // 4) * 2 + c
    flip = (y + rad) % 2
    chunk = 2 * rad + flip
    has = {
        "lo": pair > 0,
        "hi": pair < nka // 2 - 1,
        "prev": chunk > 0,
        "next": chunk < 2 * nrad - 1,
    }
    other = ka + 2 - 4 * y
    dev = {
        "lo": (jnp.maximum(jnp.where(c == 1, ka - 1, ka - 3), 0), rad),
        "hi": (jnp.minimum(jnp.where(c == 0, ka + 1, ka + 3), nka - 1), rad),
        "prev": (jnp.where(flip == 1, other, ka), jnp.where(flip == 1, rad, jnp.maximum(rad - 1, 0))),
        "next": (jnp.where(flip == 0, other, ka), jnp.where(flip == 0, rad, jnp.minimum(rad + 1, nrad - 1))),
    }
    lands = {"lo": from_hi, "hi": from_lo, "prev": from_next, "next": from_prev}
    lane = {"lo": 0, "hi": 1, "prev": 0, "next": 1}

    def copy(side, slot, k, r):
        if side in ("lo", "hi"):
            sems, at = (k_send, k_recv), r
        else:
            sems, at = (r_send, r_recv), k
        return pltpu.make_async_remote_copy(
            src_ref=wave.at[slot, k, r],
            dst_ref=lands[side].at[slot, at],
            send_sem=sems[0].at[slot, lane[side], at],
            recv_sem=sems[1].at[slot, lane[side], at],
            device_id=dev[side],
            device_id_type=MESH,
        )

    def sides_of(k, r):
        found = ["lo" if k == 0 else "hi"]
        if r == 0:
            found.append("prev")
        if r == rc - 1:
            found.append("next")
        return found

    def send(slot, k, r):
        for side in sides_of(k, r):
            @pl.when(has[side])
            def _():
                copy(side, slot, k, r).start()

    opposite = {"lo": "hi", "hi": "lo", "prev": "next", "next": "prev"}

    def receive(slot, k, r):
        for side in sides_of(k, r):
            @pl.when(has[side])
            def _():
                copy(opposite[side], slot, k, r).wait_recv()

    order = []
    for i in range(rc // 2):
        order.append((i, rc - 1 - i))

    for side, buf in (("lo", from_lo), ("hi", from_hi), ("prev", from_prev), ("next", from_next)):
        @pl.when(jnp.logical_not(has[side]))
        def _():
            buf[...] = jnp.zeros_like(buf)

    wave[0] = cur_ref[...]
    barrier = pltpu.get_barrier_semaphore()
    for side in dev:
        @pl.when(has[side])
        def _():
            pl.semaphore_signal(barrier, inc=1, device_id=dev[side], device_id_type=MESH)
    pl.semaphore_wait(barrier, sum(has[side].astype(jnp.int32) for side in dev))
    for rs in order:
        for r in rs:
            for k in range(2):
                send(0, k, r)
    wave[1] = prev_ref[...]

    def step(n, last):
        s = lax.rem(n, 2)
        t = 1 - s
        for i, rs in enumerate(order):
            for k in range(2):
                both = jnp.concatenate([wave[s, k, rs[0]], wave[s, k, rs[1]]], axis=1)
                top, low = split(both)
                ang = jnp.dot(
                    la_ref[k], jnp.concatenate([top, top, low], axis=0),
                    preferred_element_type=jnp.float32,
                )
                ptop, plow = split(ang * pot_ref[i])
                back = jnp.dot(
                    lb_ref[k], jnp.concatenate([ptop, ptop, plow], axis=0),
                    preferred_element_type=jnp.float32,
                )
                width = both.shape[1] // 2
                for e, r in enumerate(rs):
                    cols = slice(e * width, (e + 1) * width)
                    kin = jnp.dot(
                        jnp.concatenate([top[:, cols], low[:, cols]], axis=1), table_ref[...],
                        preferred_element_type=jnp.float32,
                    )
                    kin = kin[:, :width] + kin[:, width:]
                    wave[t, k, r] = (
                        diag_ref[k, r] * wave[s, k, r]
                        + scal_ref[0, r] * kin
                        + back[:, cols]
                        - scal_ref[1, r] * wave[t, k, r]
                    )
            for r in rs:
                for k in range(2):
                    receive(s, k, r)
                    ahead = wave[s, k, r + 1] if r < rc - 1 else from_next[s, k]
                    behind = wave[s, k, r - 1] if r > 0 else from_prev[s, k]
                    upper = wave[s, 1, r] if k == 0 else from_hi[s, r]
                    lower = from_lo[s, r] if k == 0 else wave[s, 0, r]
                    wave[t, k, r] = (
                        wave[t, k, r]
                        - scal_ref[2, r] * (ahead + behind)
                        + scal_ref[3, r] * (shi_ref[k] * upper + slo_ref[k] * lower)
                    )
                    if not last:
                        send(t, k, r)
        for rs in order:
            for r in rs:
                for k in range(2):
                    for side in sides_of(k, r):
                        @pl.when(has[side])
                        def _():
                            copy(side, s, k, r).wait_send()

    def body(n, carry):
        step(n, False)
        return carry

    lax.fori_loop(0, steps - 1, body, 0)
    step(steps - 1, True)


def on_device(prev_wave, cur_wave, legendre, potential, radial, rot_const, first_row):
    nka, nrad = lax.axis_size("ka"), lax.axis_size("rad")
    ka, rad = lax.axis_index("ka"), lax.axis_index("rad")
    nrot, rows, width = cur_wave.shape[1:]
    rc = rows // 2
    m = ka % 4
    hi_bit, lo_bit = m // 2, m % 2
    group = ka // 4
    odd = rad % 2
    jtop = nka - 1
    jidx = jnp.arange(nrot, dtype=jnp.int32)
    swap_a, swap_b = [], []
    for i in range(nka):
        c, b = (i % 4) // 2, i % 2
        swap_a.append((i, i - i % 4 + 2 * b + c))
        swap_b.append((i, i - i % 4 + 2 * (1 - b) + c))
    inverse_a = [(j, i) for i, j in swap_a]
    inverse_b = [(j, i) for i, j in swap_b]

    mine = (jidx >= first_row[0]).astype(jnp.float32)

    def spread(wave):
        moved = jnp.transpose(wave[0] * mine[:, None, None], (1, 0, 2))
        first = lax.dynamic_slice_in_dim(moved, (lo_bit ^ odd) * rc, rc, 0)
        second = lax.dynamic_slice_in_dim(moved, (1 - (lo_bit ^ odd)) * rc, rc, 0)
        a = lax.ppermute(first, "ka", swap_a)
        b = lax.ppermute(second, "ka", swap_b)
        return jnp.where(hi_bit == 0, jnp.stack([a, b]), jnp.stack([b, a]))

    def unspread(waves):
        a = lax.ppermute(jnp.where(hi_bit == 0, waves[0], waves[1]), "ka", inverse_a)
        b = lax.ppermute(jnp.where(hi_bit == 0, waves[1], waves[0]), "ka", inverse_b)
        whole = jnp.where((lo_bit ^ odd) == 0, jnp.concatenate([a, b]), jnp.concatenate([b, a]))
        return jnp.transpose(whole, (1, 0, 2))[None]

    packed = jnp.concatenate(
        [legendre[0] * mine[:, None], jnp.broadcast_to(first_row[0].astype(jnp.float32), (8, nrot))]
    )
    cur = spread(cur_wave)
    pa = lax.ppermute(packed, "ka", swap_a)
    pb = lax.ppermute(packed, "ka", swap_b)
    prev = spread(prev_wave)
    both = jnp.where(hi_bit == 0, jnp.stack([pa, pb]), jnp.stack([pb, pa]))
    leg = both[:, :nrot]
    firsts = both[:, nrot, 0]
    live = (jidx.astype(jnp.float32)[None, :] >= firsts[:, None]).astype(jnp.float32)

    half = hi_bit ^ odd
    local = lax.dynamic_slice_in_dim(radial, half * rc, rc, 1)
    damp = jnp.exp(-local[2])
    scal = jnp.stack([damp, damp * damp, 2.0 * COEF * damp, 2.0 * local[1] * damp])
    kval = 4 * group + 2 * lo_bit + jnp.arange(2, dtype=jnp.int32)
    qrot = (jidx * (jidx + 1)).astype(jnp.float32) / (nrot * (nrot + 1))
    pkay = (jtop * (jtop + 1) - 2 * kval * kval).astype(jnp.float32) / (nrot * (nrot + 1))
    diag = (
        rot_const[None, None, None, :] * qrot[None, None, :, None]
        + local[0][None, :, None, None] * (qrot[None, None, :, None] + pkay[:, None, None, None])
        - EMID
    )
    diag = 2.0 * damp[None, :, None, None] * (diag + 2.0 * COEF)
    s_here = live * coupling(jidx[None, :], kval[:, None], jtop, nrot)
    s_below = live * coupling(jidx[None, :], kval[:, None] - 1, jtop, nrot)
    s_here = jnp.broadcast_to(s_here[:, :, None], (2, nrot, width))
    s_below = jnp.broadcast_to(s_below[:, :, None], (2, nrot, width))

    top, low = halves(leg)
    lb = jnp.concatenate([top, low, top], axis=2)
    legt = jnp.transpose(leg, (0, 2, 1))
    top, low = halves(legt)
    la = jnp.concatenate([top, low, top], axis=2)
    top, low = halves(2.0 * sinc_table(width))
    row = jnp.concatenate([top, low], axis=1)
    table = jnp.concatenate([row, row], axis=0)
    pot = lax.dynamic_slice_in_dim(jnp.transpose(potential, (1, 0, 2)), half * rc, rc, 0)
    pot = pot * (2.0 * damp)[:, None, None]
    pot = jnp.stack([jnp.concatenate([pot[i], pot[rc - 1 - i]], axis=1) for i in range(rc // 2)])

    steps = STEPS * KICKS
    vmem = pl.BlockSpec(memory_space=pltpu.VMEM)
    point = (nrot, width)
    out = pl.pallas_call(
        functools.partial(kernel, nka, nrad, steps, rc),
        out_shape=jax.ShapeDtypeStruct((2, 2, rc) + point, jnp.float32),
        in_specs=[vmem] * 9 + [pl.BlockSpec(memory_space=pltpu.SMEM)],
        out_specs=vmem,
        scratch_shapes=[
            pltpu.VMEM((2, rc) + point, jnp.float32),
            pltpu.VMEM((2, rc) + point, jnp.float32),
            pltpu.VMEM((2, 2) + point, jnp.float32),
            pltpu.VMEM((2, 2) + point, jnp.float32),
            pltpu.SemaphoreType.DMA((2, 2, rc)),
            pltpu.SemaphoreType.DMA((2, 2, rc)),
            pltpu.SemaphoreType.DMA((2, 2, 2)),
            pltpu.SemaphoreType.DMA((2, 2, 2)),
        ],
        compiler_params=pltpu.CompilerParams(
            collective_id=0, has_side_effects=True, vmem_limit_bytes=40 * 1024 * 1024
        ),
    )(cur, prev, la, lb, table, pot, diag, s_here, s_below, scal)
    at = steps % 2
    return (unspread(out[1 - at]), unspread(out[at]))


def solution(mesh):
    placed = (
        P("ka", None, "rad", None),
        P("ka", None, "rad", None),
        P("ka", None, None),
        P(None, "rad", None),
        P(None, "rad"),
        P(),
        P("ka"),
    )
    return jax.shard_map(
        on_device,
        mesh=mesh,
        in_specs=placed,
        out_specs=(P("ka", None, "rad", None), P("ka", None, "rad", None)),
        check_vma=False,
    )
```

time: 186 us -> 103 us (0.55)
  the two profiles are of different devices: /device:TPU:1 before, /device:TPU:10 now
where the time goes in v1:
time: 103 us; the launch traced here: 102 us
  Pallas kernels  45.7 us (44%)
  waiting for transfers between devices  19.6 us (19%)
  starting transfers between devices  18.9 us (18%)
  other arithmetic  9.55 us (9%)
  local copies, waits for them, and re-layouts  6.3 us (6%)
  between operations  1.69 us (2%)
    pallas_call x1, Pallas kernels, on_device(): pl.pallas_call(functools.partial(kernel, nka, nrad, steps, rc), out_shape...  45.7 us
    ppermute x2, waiting for transfers between devices, unspread(): lax.ppermute(jnp.where(hi_bit == 0, waves[1], waves[0]), 'ka', inverse_b)  15.1 us
    ppermute x2, starting transfers between devices, spread(): a = lax.ppermute(first, 'ka', swap_a)  9.1 us
    ppermute x2, starting transfers between devices, unspread(): lax.ppermute(jnp.where(hi_bit == 0, waves[1], waves[0]), 'ka', inverse_b)  4.61 us
    ppermute x2, waiting for transfers between devices, spread(): b = lax.ppermute(second, 'ka', swap_b)  4.51 us
    select_n x2, other arithmetic, spread(): return jnp.where(hi_bit == 0, jnp.stack([a, b]), jnp.stack([b, a]))  2.91 us
    unnamed x10, local copies, waits for them, and re-layouts  2.7 us
    ppermute x2, starting transfers between devices, unspread(): lax.ppermute(jnp.where(hi_bit == 0, waves[0], waves[1]), 'ka', inverse_a)  2.32 us
  transfers between devices with their start and end apart: 10, of which 3 were waited for; matrix products, arithmetic and copies ran while one was open for 11% of the time, Pallas kernels for 0%

profile of v1, /device:TPU:10, one launch (start us, length us, event | category | flops | bytes accessed | tf_op | source)
XLA Modules:
  0.0 101.8 jit_solution(7153253208460948215)
XLA Ops:
  1.4 1.0 bitcast_multiply_fusion.2
  2.5 1.5 %collective-permute-start.5 = (f32[200,192]{1,0:T(8,128)S(1)}, f32[200,192]{1,0:T(8,128)S(1)}, u32[]{:S(2)}, u32[]{:S(2)}) collective-permute-start(f32[200,192]{1,0:T(8,128)S(1)} %concatenate.33), channel_id=1, source_target_pairs={{0,4},{2,0},{4,6},{6,2},{8,12},{10,8},{12,14},{14,10},{16,20},{18,... | collective-permute-start | bytes 460808 | tf_op jit(solution)/shard_map/ppermute | solution.py:231
  4.0 1.3 %collective-permute-start.4 = (f32[200,192]{1,0:T(8,128)S(1)}, f32[200,192]{1,0:T(8,128)}, u32[]{:S(2)}, u32[]{:S(2)}) collective-permute-start(f32[200,192]{1,0:T(8,128)S(1)} %concatenate.33), channel_id=1, source_target_pairs={{0,0},{2,4},{4,2},{6,6},{8,8},{10,12},{12,10},{14,14},{16,16},{18,... | collective-permute-start | bytes 460808 | tf_op jit(solution)/shard_map/ppermute | solution.py:230
  5.3 1.5 %bitcast_multiply_fusion = (f32[192,8,128]{2,0,1:T(8,128)S(1)}, f32[192,8,128]{2,0,1:T(8,128)S(1)}) fusion(f32[1,192,8,128]{3,2,1,0:T(8,128)S(1)} %copy-done.1, f32[192]{0:T(256)S(1)} %compare_convert_fusion, f32[1,192,8,128]{3,2,1,0:T(8,128)} %param.8), kind=kLoop, calls=%fused_computation.6 | loop fusion | flops 393216 | bytes 3146496 | tf_op jit(solution)/shard_map/mul | solution.py:213
  6.8 0.8 dynamic-slice_bitcast_fusion.1
  7.7 4.6 %collective-permute-start.2 = (f32[4,192,128]{2,1,0:T(8,128)}, f32[4,192,128]{2,1,0:T(8,128)}, u32[]{:S(2)}, u32[]{:S(2)}) collective-permute-start(f32[4,192,128]{2,1,0:T(8,128)} %get-tuple-element.12), channel_id=1, source_target_pairs={{0,0},{2,4},{4,2},{6,6},{8,8},{10,12},{12,10},{14,14},{16,16},{18,... | collective-permute-start | bytes 1179656 | tf_op jit(solution)/shard_map/ppermute | solution.py:216
  12.3 0.9 dynamic-slice_bitcast_fusion.3
  13.2 4.5 %collective-permute-start = (f32[4,192,128]{2,1,0:T(8,128)}, f32[4,192,128]{2,1,0:T(8,128)}, u32[]{:S(2)}, u32[]{:S(2)}) collective-permute-start(f32[4,192,128]{2,1,0:T(8,128)} %get-tuple-element.14), channel_id=1, source_target_pairs={{0,0},{2,4},{4,2},{6,6},{8,8},{10,12},{12,10},{14,14},{16,16},{18,... | collective-permute-start | bytes 1179656 | tf_op jit(solution)/shard_map/ppermute | solution.py:216
  18.9 1.1 %maximum_select_fusion.4 = f32[2,200,192]{2,1,0:T(8,128)S(1)} fusion(f32[1,200,192]{2,1,0:T(8,128)S(1)} %bitcast.60, f32[1,200,192]{2,1,0:T(8,128)} %bitcast.12, pred[]{:T(512)S(6)} %eq.28), kind=kLoop, calls=%fused_computation.15 | loop fusion | flops 230400 | bytes 614401 | tf_op jit(solution)/shard_map/jit(_where)/select_n | solution.py:233
  20.1 0.9 pad_maximum_fusion
  21.2 1.3 %copy.18.la_ref = bf16[2,192,576]{2,1,0:T(8,128)(2,1)S(1)} copy(bf16[2,192,576]{1,2,0:T(8,128)(2,1)} %pad_maximum_fusion) | data formatting | bytes 884736 | tf_op jit(solution)/shard_map/concatenate | solution.py:260
  22.7 1.4 %maximum_select_fusion.1.prev_ref = f32[2,4,192,128]{3,2,1,0:T(8,128)S(1)} fusion(f32[1,4,192,128]{3,2,1,0:T(8,128)} %bitcast.10, f32[1,4,192,128]{3,2,1,0:T(8,128)} %bitcast.8, pred[]{:T(512)S(6)} %eq.28), kind=kLoop, calls=%fused_computation.1 | loop fusion | flops 589824 | bytes 1572865 | tf_op jit(solution)/shard_map/jit(_where)/select_n | solution.py:218
  24.1 4.5 %collective-permute-done.1 = f32[4,192,128]{2,1,0:T(8,128)} collective-permute-done((f32[4,192,128]{2,1,0:T(8,128)}, f32[4,192,128]{2,1,0:T(8,128)}, u32[]{:S(2)}, u32[]{:S(2)}) %collective-permute-start.1) | collective-permute-done | bytes 393248 | tf_op jit(solution)/shard_map/ppermute | solution.py:217
  28.6 1.5 %maximum_select_fusion.cur_ref = f32[2,4,192,128]{3,2,1,0:T(8,128)S(1)} fusion(f32[1,4,192,128]{3,2,1,0:T(8,128)} %bitcast.5, f32[1,4,192,128]{3,2,1,0:T(8,128)} %bitcast.3, pred[]{:T(512)S(6)} %eq.28), kind=kLoop, calls=%fused_computation | loop fusion | flops 589824 | bytes 1572865 | tf_op jit(solution)/shard_map/jit(_where)/select_n | solution.py:218
  30.3 45.7 %shard_map.86 = f32[2,2,4,192,128]{4,3,2,1,0:T(8,128)S(1)} custom-call(f32[2,4,192,128]{3,2,1,0:T(8,128)S(1)} %maximum_select_fusion.cur_ref, f32[2,4,192,128]{3,2,1,0:T(8,128)S(1)} %maximum_select_fusion.1.prev_ref, bf16[2,192,576]{2,1,0:T(8,128)(2,1)S(1)} %copy.18.la_ref, bf16[2,192,576]{2,1,0:T(8,128)(2,1)S(1)} %pad_maximum_fusion.1.lb_ref, ...), custom_call_target="tpu_custom_call" | custom-call | tf_op jit(solution)/shard_map/pallas_call | solution.py:271
  76.0 0.9 select_bitcast_fusion.1
  76.9 1.6 %collective-permute-start.8 = (f32[4,192,128]{2,1,0:T(8,128)}, f32[4,192,128]{2,1,0:T(8,128)S(1)}, u32[]{:S(2)}, u32[]{:S(2)}) collective-permute-start(f32[4,192,128]{2,1,0:T(8,128)} %get-tuple-element.8), channel_id=1, source_target_pairs={{0,0},{4,2},{2,4},{6,6},{8,8},{12,10},{10,12},{14,14},{16,16},{20,... | collective-permute-start | bytes 1179656 | tf_op jit(solution)/shard_map/ppermute | solution.py:221
  78.6 1.6 %collective-permute-start.9 = (f32[4,192,128]{2,1,0:T(8,128)S(1)}, f32[4,192,128]{2,1,0:T(8,128)S(1)}, u32[]{:S(2)}, u32[]{:S(2)}) collective-permute-start(f32[4,192,128]{2,1,0:T(8,128)S(1)} %get-tuple-element.9), channel_id=1, source_target_pairs={{4,0},{0,2},{6,4},{2,6},{12,8},{8,10},{14,12},{10,14},{20,16},{16,... | collective-permute-start | bytes 1179656 | tf_op jit(solution)/shard_map/ppermute | solution.py:222
  80.2 0.7 collective-permute-start.6
  80.9 3.0 %collective-permute-start.7 = (f32[4,192,128]{2,1,0:T(8,128)S(1)}, f32[4,192,128]{2,1,0:T(8,128)S(1)}, u32[]{:S(2)}, u32[]{:S(2)}) collective-permute-start(f32[4,192,128]{2,1,0:T(8,128)S(1)} %get-tuple-element.11), channel_id=1, source_target_pairs={{4,0},{0,2},{6,4},{2,6},{12,8},{8,10},{14,12},{10,14},{20,16},{16,... | collective-permute-start | bytes 1179656 | tf_op jit(solution)/shard_map/ppermute | solution.py:222
  83.9 8.1 %collective-permute-done.9 = f32[4,192,128]{2,1,0:T(8,128)S(1)} collective-permute-done((f32[4,192,128]{2,1,0:T(8,128)S(1)}, f32[4,192,128]{2,1,0:T(8,128)S(1)}, u32[]{:S(2)}, u32[]{:S(2)}) %collective-permute-start.9) | collective-permute-done | bytes 393248 | tf_op jit(solution)/shard_map/ppermute | solution.py:222
  92.0 1.3 %copy.20 = f32[1,192,8,128]{3,2,1,0:T(8,128)} copy(f32[1,192,8,128]{3,1,2,0:T(8,128)S(1)} %fusion.1) | data formatting | bytes 1572864
  93.3 7.0 %collective-permute-done.7 = f32[4,192,128]{2,1,0:T(8,128)S(1)} collective-permute-done((f32[4,192,128]{2,1,0:T(8,128)S(1)}, f32[4,192,128]{2,1,0:T(8,128)S(1)}, u32[]{:S(2)}, u32[]{:S(2)}) %collective-permute-start.7) | collective-permute-done | bytes 393248 | tf_op jit(solution)/shard_map/ppermute | solution.py:222
  100.4 1.3 %copy.19 = f32[1,192,8,128]{3,2,1,0:T(8,128)} copy(f32[1,192,8,128]{3,1,2,0:T(8,128)S(1)} %fusion) | data formatting | bytes 1572864
  (48 shorter events, 1.9 us)
Async XLA Ops:
  0.6 17.5 %copy-start = (f32[192,8,128]{2,1,0:T(8,128)S(1)}, f32[192,8,128]{2,1,0:T(8,128)}, u32[]{:S(2)}) copy-start(f32[192,8,128]{2,1,0:T(8,128)} %param.10) | copy-start | bytes 2359300
  0.6 4.7 %copy-start.1 = (f32[1,192,8,128]{3,2,1,0:T(8,128)S(1)}, f32[1,192,8,128]{3,2,1,0:T(8,128)}, u32[]{:S(2)}) copy-start(f32[1,192,8,128]{3,2,1,0:T(8,128)} %param.7) | copy-start | bytes 2359300
  2.5 16.3 %collective-permute-start.5 = (f32[200,192]{1,0:T(8,128)S(1)}, f32[200,192]{1,0:T(8,128)S(1)}, u32[]{:S(2)}, u32[]{:S(2)}) collective-permute-start(f32[200,192]{1,0:T(8,128)S(1)} %concatenate.33), channel_id=1, source_target_pairs={{0,4},{2,0},{4,6},{6,2},{8,12},{10,8},{12,14},{14,10},{16,20},{18,... | collective-permute-start | bytes 460808 | tf_op jit(solution)/shard_map/ppermute | solution.py:231
  4.0 14.8 %collective-permute-start.4 = (f32[200,192]{1,0:T(8,128)S(1)}, f32[200,192]{1,0:T(8,128)}, u32[]{:S(2)}, u32[]{:S(2)}) collective-permute-start(f32[200,192]{1,0:T(8,128)S(1)} %concatenate.33), channel_id=1, source_target_pairs={{0,0},{2,4},{4,2},{6,6},{8,8},{10,12},{12,10},{14,14},{16,16},{18,... | collective-permute-start | bytes 460808 | tf_op jit(solution)/shard_map/ppermute | solution.py:230
  7.7 10.2 %copy-start.2 = (f32[3,8]{1,0:T(4,128)S(1)}, f32[3,8]{1,0:T(4,128)}, u32[]{:S(2)}) copy-start(f32[3,8]{1,0:T(4,128)} %param.11) | copy-start | bytes 292
  7.7 10.3 %copy-start.3 = (f32[128]{0:T(128)S(1)}, f32[128]{0:T(128)}, u32[]{:S(2)}) copy-start(f32[128]{0:T(128)} %param.12) | copy-start | bytes 1540
  7.7 15.0 %collective-permute-start.2 = (f32[4,192,128]{2,1,0:T(8,128)}, f32[4,192,128]{2,1,0:T(8,128)}, u32[]{:S(2)}, u32[]{:S(2)}) collective-permute-start(f32[4,192,128]{2,1,0:T(8,128)} %get-tuple-element.12), channel_id=1, source_target_pairs={{0,0},{2,4},{4,2},{6,6},{8,8},{10,12},{12,10},{14,14},{16,16},{18,... | collective-permute-start | bytes 1179656 | tf_op jit(solution)/shard_map/ppermute | solution.py:216
  12.3 10.4 %collective-permute-start.3 = (f32[4,192,128]{2,1,0:T(8,128)S(1)}, f32[4,192,128]{2,1,0:T(8,128)}, u32[]{:S(2)}, u32[]{:S(2)}) collective-permute-start(f32[4,192,128]{2,1,0:T(8,128)S(1)} %get-tuple-element.13), channel_id=1, source_target_pairs={{0,4},{2,0},{4,6},{6,2},{8,12},{10,8},{12,14},{14,10},{16,20},{18,... | collective-permute-start | bytes 1179656 | tf_op jit(solution)/shard_map/ppermute | solution.py:217
  13.2 10.9 %collective-permute-start = (f32[4,192,128]{2,1,0:T(8,128)}, f32[4,192,128]{2,1,0:T(8,128)}, u32[]{:S(2)}, u32[]{:S(2)}) collective-permute-start(f32[4,192,128]{2,1,0:T(8,128)} %get-tuple-element.14), channel_id=1, source_target_pairs={{0,0},{2,4},{4,2},{6,6},{8,8},{10,12},{12,10},{14,14},{16,16},{18,... | collective-permute-start | bytes 1179656 | tf_op jit(solution)/shard_map/ppermute | solution.py:216
  18.8 9.8 %collective-permute-start.1 = (f32[4,192,128]{2,1,0:T(8,128)}, f32[4,192,128]{2,1,0:T(8,128)}, u32[]{:S(2)}, u32[]{:S(2)}) collective-permute-start(f32[4,192,128]{2,1,0:T(8,128)} %get-tuple-element.15), channel_id=1, source_target_pairs={{0,4},{2,0},{4,6},{6,2},{8,12},{10,8},{12,14},{14,10},{16,20},{18,... | collective-permute-start | bytes 1179656 | tf_op jit(solution)/shard_map/ppermute | solution.py:217
  76.9 6.9 %collective-permute-start.8 = (f32[4,192,128]{2,1,0:T(8,128)}, f32[4,192,128]{2,1,0:T(8,128)S(1)}, u32[]{:S(2)}, u32[]{:S(2)}) collective-permute-start(f32[4,192,128]{2,1,0:T(8,128)} %get-tuple-element.8), channel_id=1, source_target_pairs={{0,0},{4,2},{2,4},{6,6},{8,8},{12,10},{10,12},{14,14},{16,16},{20,... | collective-permute-start | bytes 1179656 | tf_op jit(solution)/shard_map/ppermute | solution.py:221
  78.6 13.4 %collective-permute-start.9 = (f32[4,192,128]{2,1,0:T(8,128)S(1)}, f32[4,192,128]{2,1,0:T(8,128)S(1)}, u32[]{:S(2)}, u32[]{:S(2)}) collective-permute-start(f32[4,192,128]{2,1,0:T(8,128)S(1)} %get-tuple-element.9), channel_id=1, source_target_pairs={{4,0},{0,2},{6,4},{2,6},{12,8},{8,10},{14,12},{10,14},{20,16},{16,... | collective-permute-start | bytes 1179656 | tf_op jit(solution)/shard_map/ppermute | solution.py:222
  80.2 13.2 %collective-permute-start.6 = (f32[4,192,128]{2,1,0:T(8,128)S(1)}, f32[4,192,128]{2,1,0:T(8,128)S(1)}, u32[]{:S(2)}, u32[]{:S(2)}) collective-permute-start(f32[4,192,128]{2,1,0:T(8,128)S(1)} %get-tuple-element.10), channel_id=1, source_target_pairs={{0,0},{4,2},{2,4},{6,6},{8,8},{12,10},{10,12},{14,14},{16,16},{20,... | collective-permute-start | bytes 1179656 | tf_op jit(solution)/shard_map/ppermute | solution.py:221
  80.9 19.5 %collective-permute-start.7 = (f32[4,192,128]{2,1,0:T(8,128)S(1)}, f32[4,192,128]{2,1,0:T(8,128)S(1)}, u32[]{:S(2)}, u32[]{:S(2)}) collective-permute-start(f32[4,192,128]{2,1,0:T(8,128)S(1)} %get-tuple-element.11), channel_id=1, source_target_pairs={{4,0},{0,2},{6,4},{2,6},{12,8},{8,10},{14,12},{10,14},{20,16},{16,... | collective-permute-start | bytes 1179656 | tf_op jit(solution)/shard_map/ppermute | solution.py:222

commit v2 on v1

--- a/solution.py
+++ b/solution.py
@@ -43,10 +43,11 @@
 
 def kernel(
     nka, nrad, steps, rc,
-    cur_ref, prev_ref, la_ref, lb_ref, table_ref, pot_ref, diag_ref, shi_ref, slo_ref, scal_ref,
-    wave,
+    cur_ref, prev_ref, leg_ref, table_ref, pot_ref, diag_ref, here_ref, below_ref, scal_ref,
+    prev_out, cur_out,
+    wave, legs, la_ref, lb_ref, shi_ref, slo_ref,
     from_lo, from_hi, from_prev, from_next,
-    k_send, k_recv, r_send, r_recv,
+    k_send, k_recv, r_send, r_recv, in_send, in_recv, old_send, old_recv, new_send, new_recv,
 ):
     ka, rad = lax.axis_index("ka"), lax.axis_index("rad")
     m = ka % 4
@@ -106,6 +107,72 @@
             def _():
                 copy(opposite[side], slot, k, r).wait_recv()
 
+    base = ka - m
+    odd = rad % 2
+    nrot = wave.shape[3]
+
+    def give(which, part):
+        dest = base + 2 * part + y
+        source = (cur_ref, prev_ref, leg_ref)[which]
+        if which < 2:
+            source = source.at[pl.ds(((part + odd) % 2) * rc, rc)]
+            target = wave.at[which, c]
+        else:
+            target = legs.at[c]
+        remote = pltpu.make_async_remote_copy(
+            src_ref=source, dst_ref=target,
+            send_sem=in_send.at[which, part], recv_sem=in_recv.at[which, c],
+            device_id=(dest, rad), device_id_type=MESH,
+        )
+        return dest, source, target, remote
+
+    def give_start(which):
+        for part in range(2):
+            dest, source, target, remote = give(which, part)
+
+            @pl.when(dest != ka)
+            def _():
+                remote.start()
+
+            @pl.when(dest == ka)
+            def _():
+                target[...] = source[...]
+
+    def give_sent(which):
+        for part in range(2):
+            dest, _, _, remote = give(which, part)
+
+            @pl.when(dest != ka)
+            def _():
+                remote.wait_send()
+
+    def take(which):
+        for k in range(2):
+            @pl.when(base + 2 * c + k != ka)
+            def _():
+                target = legs.at[k] if which == 2 else wave.at[which, k]
+                pltpu.make_async_remote_copy(
+                    src_ref=target, dst_ref=target,
+                    send_sem=in_send.at[which, 0], recv_sem=in_recv.at[which, k],
+                    device_id=(other, rad), device_id_type=MESH,
+                ).wait_recv()
+
+    def back_old(slot, k):
+        dest = base + 2 * c + k
+        return dest, pltpu.make_async_remote_copy(
+            src_ref=wave.at[slot, k], dst_ref=prev_out.at[pl.ds(flip * rc, rc)],
+            send_sem=old_send.at[k], recv_sem=old_recv.at[y],
+            device_id=(dest, rad), device_id_type=MESH,
+        )
+
+    def back_new(slot, k, r):
+        dest = base + 2 * c + k
+        return dest, pltpu.make_async_remote_copy(
+            src_ref=wave.at[slot, k, r], dst_ref=cur_out.at[flip * rc + r],
+            send_sem=new_send.at[k, r], recv_sem=new_recv.at[y, r],
+            device_id=(dest, rad), device_id_type=MESH,
+        )
+
     order = []
     for i in range(rc // 2):
         order.append((i, rc - 1 - i))
@@ -115,18 +182,38 @@
         def _():
             buf[...] = jnp.zeros_like(buf)
 
-    wave[0] = cur_ref[...]
     barrier = pltpu.get_barrier_semaphore()
     for side in dev:
         @pl.when(has[side])
         def _():
             pl.semaphore_signal(barrier, inc=1, device_id=dev[side], device_id_type=MESH)
-    pl.semaphore_wait(barrier, sum(has[side].astype(jnp.int32) for side in dev))
+    for away in range(1, 4):
+        pl.semaphore_signal(
+            barrier, inc=1, device_id=(base + (m + away) % 4, rad), device_id_type=MESH
+        )
+    pl.semaphore_wait(barrier, 3 + sum(has[side].astype(jnp.int32) for side in dev))
+
+    give_start(0)
+    give_start(2)
+    take(0)
     for rs in order:
         for r in rs:
             for k in range(2):
                 send(0, k, r)
-    wave[1] = prev_ref[...]
+    give_start(1)
+    take(2)
+    for k in range(2):
+        leg = legs[k, :nrot]
+        top, low = split(leg)
+        lb_ref[k] = jnp.concatenate([top, low, top], axis=1)
+        top, low = split(leg.T)
+        la_ref[k] = jnp.concatenate([top, low, top], axis=1)
+        first = legs[k, nrot : nrot + 1, : wave.shape[4]]
+        at_row = lax.broadcasted_iota(jnp.int32, wave.shape[3:], 0).astype(jnp.float32)
+        live = (at_row >= first).astype(jnp.float32)
+        shi_ref[k] = live * here_ref[k]
+        slo_ref[k] = live * below_ref[k]
+    take(1)
 
     def step(n, last):
         s = lax.rem(n, 2)
@@ -172,6 +259,16 @@
                     )
                     if not last:
                         send(t, k, r)
+                    else:
+                        dest, remote = back_new(t, k, r)
+
+                        @pl.when(dest != ka)
+                        def _():
+                            remote.start()
+
+                        @pl.when(dest == ka)
+                        def _():
+                            cur_out[flip * rc + r] = wave[t, k, r]
         for rs in order:
             for r in rs:
                 for k in range(2):
@@ -185,7 +282,44 @@
         return carry
 
     lax.fori_loop(0, steps - 1, body, 0)
+    slot = (steps - 1) % 2
+    for k in range(2):
+        dest, remote = back_old(slot, k)
+
+        @pl.when(dest != ka)
+        def _():
+            remote.start()
+
+        @pl.when(dest == ka)
+        def _():
+            prev_out[pl.ds(flip * rc, rc)] = wave[slot, k]
     step(steps - 1, True)
+    for which in range(3):
+        give_sent(which)
+    for k in range(2):
+        dest, remote = back_old(slot, k)
+
+        @pl.when(dest != ka)
+        def _():
+            remote.wait_send()
+            for r in range(rc):
+                back_new(1 - slot, k, r)[1].wait_send()
+    for part in range(2):
+        at = ((part + odd) % 2) * rc
+
+        @pl.when(base + 2 * part + y != ka)
+        def _():
+            pltpu.make_async_remote_copy(
+                src_ref=wave.at[slot, 0], dst_ref=prev_out.at[pl.ds(at, rc)],
+                send_sem=old_send.at[0], recv_sem=old_recv.at[part],
+                device_id=(other, rad), device_id_type=MESH,
+            ).wait_recv()
+            for r in range(rc):
+                pltpu.make_async_remote_copy(
+                    src_ref=wave.at[1 - slot, 0, r], dst_ref=cur_out.at[at + r],
+                    send_sem=new_send.at[0, r], recv_sem=new_recv.at[part, r],
+                    device_id=(other, rad), device_id_type=MESH,
+                ).wait_recv()
 
 
 def on_device(prev_wave, cur_wave, legendre, potential, radial, rot_const, first_row):
@@ -199,41 +333,12 @@
     odd = rad % 2
     jtop = nka - 1
     jidx = jnp.arange(nrot, dtype=jnp.int32)
-    swap_a, swap_b = [], []
-    for i in range(nka):
-        c, b = (i % 4) // 2, i % 2
-        swap_a.append((i, i - i % 4 + 2 * b + c))
-        swap_b.append((i, i - i % 4 + 2 * (1 - b) + c))
-    inverse_a = [(j, i) for i, j in swap_a]
-    inverse_b = [(j, i) for i, j in swap_b]
-
     mine = (jidx >= first_row[0]).astype(jnp.float32)
-
-    def spread(wave):
-        moved = jnp.transpose(wave[0] * mine[:, None, None], (1, 0, 2))
-        first = lax.dynamic_slice_in_dim(moved, (lo_bit ^ odd) * rc, rc, 0)
-        second = lax.dynamic_slice_in_dim(moved, (1 - (lo_bit ^ odd)) * rc, rc, 0)
-        a = lax.ppermute(first, "ka", swap_a)
-        b = lax.ppermute(second, "ka", swap_b)
-        return jnp.where(hi_bit == 0, jnp.stack([a, b]), jnp.stack([b, a]))
-
-    def unspread(waves):
-        a = lax.ppermute(jnp.where(hi_bit == 0, waves[0], waves[1]), "ka", inverse_a)
-        b = lax.ppermute(jnp.where(hi_bit == 0, waves[1], waves[0]), "ka", inverse_b)
-        whole = jnp.where((lo_bit ^ odd) == 0, jnp.concatenate([a, b]), jnp.concatenate([b, a]))
-        return jnp.transpose(whole, (1, 0, 2))[None]
-
+    cur = jnp.transpose(cur_wave[0] * mine[:, None, None], (1, 0, 2))
+    prev = jnp.transpose(prev_wave[0] * mine[:, None, None], (1, 0, 2))
     packed = jnp.concatenate(
         [legendre[0] * mine[:, None], jnp.broadcast_to(first_row[0].astype(jnp.float32), (8, nrot))]
     )
-    cur = spread(cur_wave)
-    pa = lax.ppermute(packed, "ka", swap_a)
-    pb = lax.ppermute(packed, "ka", swap_b)
-    prev = spread(prev_wave)
-    both = jnp.where(hi_bit == 0, jnp.stack([pa, pb]), jnp.stack([pb, pa]))
-    leg = both[:, :nrot]
-    firsts = both[:, nrot, 0]
-    live = (jidx.astype(jnp.float32)[None, :] >= firsts[:, None]).astype(jnp.float32)
 
     half = hi_bit ^ odd
     local = lax.dynamic_slice_in_dim(radial, half * rc, rc, 1)
@@ -248,16 +353,11 @@
         - EMID
     )
     diag = 2.0 * damp[None, :, None, None] * (diag + 2.0 * COEF)
-    s_here = live * coupling(jidx[None, :], kval[:, None], jtop, nrot)
-    s_below = live * coupling(jidx[None, :], kval[:, None] - 1, jtop, nrot)
+    s_here = coupling(jidx[None, :], kval[:, None], jtop, nrot)
+    s_below = coupling(jidx[None, :], kval[:, None] - 1, jtop, nrot)
     s_here = jnp.broadcast_to(s_here[:, :, None], (2, nrot, width))
     s_below = jnp.broadcast_to(s_below[:, :, None], (2, nrot, width))
 
-    top, low = halves(leg)
-    lb = jnp.concatenate([top, low, top], axis=2)
-    legt = jnp.transpose(leg, (0, 2, 1))
-    top, low = halves(legt)
-    la = jnp.concatenate([top, low, top], axis=2)
     top, low = halves(2.0 * sinc_table(width))
     row = jnp.concatenate([top, low], axis=1)
     table = jnp.concatenate([row, row], axis=0)
@@ -268,27 +368,32 @@
     steps = STEPS * KICKS
     vmem = pl.BlockSpec(memory_space=pltpu.VMEM)
     point = (nrot, width)
-    out = pl.pallas_call(
+    whole = jax.ShapeDtypeStruct((rows,) + point, jnp.float32)
+    sem = pltpu.SemaphoreType.DMA
+    prev_out, cur_out = pl.pallas_call(
         functools.partial(kernel, nka, nrad, steps, rc),
-        out_shape=jax.ShapeDtypeStruct((2, 2, rc) + point, jnp.float32),
-        in_specs=[vmem] * 9 + [pl.BlockSpec(memory_space=pltpu.SMEM)],
-        out_specs=vmem,
+        out_shape=(whole, whole),
+        in_specs=[vmem] * 8 + [pl.BlockSpec(memory_space=pltpu.SMEM)],
+        out_specs=(vmem, vmem),
         scratch_shapes=[
+            pltpu.VMEM((2, 2, rc) + point, jnp.float32),
+            pltpu.VMEM((2, nrot + 8, nrot), jnp.float32),
+            pltpu.VMEM((2, nrot, 3 * nrot), jnp.bfloat16),
+            pltpu.VMEM((2, nrot, 3 * nrot), jnp.bfloat16),
+            pltpu.VMEM((2,) + point, jnp.float32),
+            pltpu.VMEM((2,) + point, jnp.float32),
             pltpu.VMEM((2, rc) + point, jnp.float32),
             pltpu.VMEM((2, rc) + point, jnp.float32),
             pltpu.VMEM((2, 2) + point, jnp.float32),
             pltpu.VMEM((2, 2) + point, jnp.float32),
-            pltpu.SemaphoreType.DMA((2, 2, rc)),
-            pltpu.SemaphoreType.DMA((2, 2, rc)),
-            pltpu.SemaphoreType.DMA((2, 2, 2)),
-            pltpu.SemaphoreType.DMA((2, 2, 2)),
+            sem((2, 2, rc)), sem((2, 2, rc)), sem((2, 2, 2)), sem((2, 2, 2)),
+            sem((3, 2)), sem((3, 2)), sem((2,)), sem((2,)), sem((2, rc)), sem((2, rc)),
         ],
         compiler_params=pltpu.CompilerParams(
             collective_id=0, has_side_effects=True, vmem_limit_bytes=40 * 1024 * 1024
         ),
-    )(cur, prev, la, lb, table, pot, diag, s_here, s_below, scal)
-    at = steps % 2
-    return (unspread(out[1 - at]), unspread(out[at]))
+    )(cur, prev, packed, table, pot, diag, s_here, s_below, scal)
+    return (jnp.transpose(prev_out, (1, 0, 2))[None], jnp.transpose(cur_out, (1, 0, 2))[None])
 
 
 def solution(mesh):

time: 103 us -> 93.5 us (0.908)
  the two profiles are of different devices: /device:TPU:10 before, /device:TPU:1 now
where the time goes in v2:
time: 93.5 us; the launch traced here: 91.7 us
  Pallas kernels  82.6 us (88%)
  local copies, waits for them, and re-layouts  6.06 us (6%)
  between operations  1.61 us (2%)
  other arithmetic  1.35 us (1%)
    pallas_call x1, Pallas kernels, on_device(): pl.pallas_call(functools.partial(kernel, nka, nrad, steps, rc), out_shape...  82.6 us
    unnamed x14, local copies, waits for them, and re-layouts  5.65 us

profile of v2, /device:TPU:1, one launch (start us, length us, event | category | flops | bytes accessed | tf_op | source)
XLA Modules:
  0.0 91.7 jit_solution(10878969090272754016)
XLA Ops:
  0.6 0.0 copy-start
  1.5 0.1 sqrt_multiply_fusion
  1.6 0.0 copy-start.4
  1.6 0.1 broadcast_add_fusion
  1.7 0.6 copy-done.4
  2.3 0.1 constant_dynamic-slice_fusion
  2.4 0.1 broadcast_multiply_fusion.1
  2.4 0.1 reduce-precision_convert_fusion
  2.5 0.0 copy-start.5
  2.6 0.6 copy-done.5
  3.2 0.1 broadcast_multiply_fusion
  3.3 0.1 broadcast_in_dim.13.below_ref
  3.4 0.1 broadcast_in_dim.12.here_ref
  3.5 0.7 copy-done.3
  4.2 0.1 bitcast_multiply_fusion.2
  4.3 0.1 constant_dynamic-slice_fusion.1
  4.4 0.1 fusion.2
  4.7 0.3 add_multiply_fusion.diag_ref
  4.9 0.8 copy-done.1
  5.7 0.2 copy-done.2
  6.0 0.4 fusion
  6.3 82.6 %shard_map.86 = (f32[8,192,128]{2,1,0:T(8,128)S(1)}, f32[8,192,128]{2,1,0:T(8,128)S(1)}) custom-call(f32[8,192,128]{2,1,0:T(8,128)S(1)} %get-tuple-element.19.cur_ref, f32[8,192,128]{2,1,0:T(8,128)S(1)} %get-tuple-element.18.prev_ref, f32[200,192]{1,0:T(8,128)S(1)} %concatenate.15.leg_ref, bf16[256,256]{1,0:T(8,128)(2,1)S(1)} %maximum_maximum_fusion.table_ref, ...), custom_call_target="tpu_custom_call" | custom-call | tf_op jit(solution)/shard_map/pallas_call | solution.py:373
  89.0 1.3 %copy.12 = f32[1,192,8,128]{3,2,1,0:T(8,128)} copy(f32[1,192,8,128]{3,1,2,0:T(8,128)S(1)} %bitcast.42) | data formatting | bytes 1572864
  90.3 1.3 %copy.13 = f32[1,192,8,128]{3,2,1,0:T(8,128)} copy(f32[1,192,8,128]{3,1,2,0:T(8,128)S(1)} %bitcast.41) | data formatting | bytes 1572864
  (18 shorter events, 0.2 us)
Async XLA Ops:
  0.6 3.7 %copy-start = (f32[192,8,128]{2,1,0:T(8,128)S(1)}, f32[192,8,128]{2,1,0:T(8,128)}, u32[]{:S(2)}) copy-start(f32[192,8,128]{2,1,0:T(8,128)} %param.10) | copy-start | bytes 2359300
  1.6 0.7 copy-start.4
  2.5 0.7 copy-start.5
  3.3 0.9 %copy-start.3 = (f32[1,192,192]{2,1,0:T(8,128)S(1)}, f32[1,192,192]{2,1,0:T(8,128)}, u32[]{:S(2)}) copy-start(f32[1,192,192]{2,1,0:T(8,128)} %param.9) | copy-start | bytes 442372
  4.6 1.1 %copy-start.1 = (f32[1,192,8,128]{3,2,1,0:T(8,128)S(1)}, f32[1,192,8,128]{3,2,1,0:T(8,128)}, u32[]{:S(2)}) copy-start(f32[1,192,8,128]{3,2,1,0:T(8,128)} %param.7) | copy-start | bytes 2359300
  4.6 1.4 %copy-start.2 = (f32[1,192,8,128]{3,2,1,0:T(8,128)S(1)}, f32[1,192,8,128]{3,2,1,0:T(8,128)}, u32[]{:S(2)}) copy-start(f32[1,192,8,128]{3,2,1,0:T(8,128)} %param.8) | copy-start | bytes 2359300

commit v3 on v2

--- a/solution.py
+++ b/solution.py
@@ -47,7 +47,7 @@
     prev_out, cur_out,
     wave, legs, la_ref, lb_ref, shi_ref, slo_ref,
     from_lo, from_hi, from_prev, from_next,
-    k_send, k_recv, r_send, r_recv, in_send, in_recv, old_send, old_recv, new_send, new_recv,
+    k_send, k_recv, r_send, r_recv, in_send, in_recv, old_in_send, old_in_recv, old_send, old_recv, new_send, new_recv,
 ):
     ka, rad = lax.axis_index("ka"), lax.axis_index("rad")
     m = ka % 4
@@ -86,12 +86,12 @@
         )
 
     def sides_of(k, r):
-        found = ["lo" if k == 0 else "hi"]
+        found = []
         if r == 0:
             found.append("prev")
         if r == rc - 1:
             found.append("next")
-        return found
+        return found + ["lo" if k == 0 else "hi"]
 
     def send(slot, k, r):
         for side in sides_of(k, r):
@@ -113,10 +113,10 @@
 
     def give(which, part):
         dest = base + 2 * part + y
-        source = (cur_ref, prev_ref, leg_ref)[which]
-        if which < 2:
-            source = source.at[pl.ds(((part + odd) % 2) * rc, rc)]
-            target = wave.at[which, c]
+        source = leg_ref
+        if which == 0:
+            source = cur_ref.at[pl.ds(((part + odd) % 2) * rc, rc)]
+            target = wave.at[0, c]
         else:
             target = legs.at[c]
         remote = pltpu.make_async_remote_copy(
@@ -126,6 +126,26 @@
         )
         return dest, source, target, remote
 
+    def give_prev(part, r):
+        dest = base + 2 * part + y
+        source = prev_ref.at[((part + odd) % 2) * rc + r]
+        target = wave.at[1, c, r]
+        remote = pltpu.make_async_remote_copy(
+            src_ref=source, dst_ref=target,
+            send_sem=old_in_send.at[part, r], recv_sem=old_in_recv.at[c, r],
+            device_id=(dest, rad), device_id_type=MESH,
+        )
+        return dest, source, target, remote
+
+    def take_prev(k, r):
+        @pl.when(base + 2 * c + k != ka)
+        def _():
+            pltpu.make_async_remote_copy(
+                src_ref=wave.at[1, k, r], dst_ref=wave.at[1, k, r],
+                send_sem=old_in_send.at[0, r], recv_sem=old_in_recv.at[k, r],
+                device_id=(other, rad), device_id_type=MESH,
+            ).wait_recv()
+
     def give_start(which):
         for part in range(2):
             dest, source, target, remote = give(which, part)
@@ -197,10 +217,21 @@
     give_start(2)
     take(0)
     for rs in order:
+        for k in range(2):
+            for r in rs:
+                send(0, k, r)
+    for rs in order:
         for r in rs:
-            for k in range(2):
-                send(0, k, r)
-    give_start(1)
+            for part in range(2):
+                dest, source, target, remote = give_prev(part, r)
+
+                @pl.when(dest != ka)
+                def _():
+                    remote.start()
+
+                @pl.when(dest == ka)
+                def _():
+                    target[...] = source[...]
     take(2)
     for k in range(2):
         leg = legs[k, :nrot]
@@ -213,9 +244,7 @@
         live = (at_row >= first).astype(jnp.float32)
         shi_ref[k] = live * here_ref[k]
         slo_ref[k] = live * below_ref[k]
-    take(1)
-
-    def step(n, last):
+    def step(n, last, first=False):
         s = lax.rem(n, 2)
         t = 1 - s
         for i, rs in enumerate(order):
@@ -239,14 +268,16 @@
                         preferred_element_type=jnp.float32,
                     )
                     kin = kin[:, :width] + kin[:, width:]
+                    if first:
+                        take_prev(k, r)
                     wave[t, k, r] = (
                         diag_ref[k, r] * wave[s, k, r]
                         + scal_ref[0, r] * kin
                         + back[:, cols]
                         - scal_ref[1, r] * wave[t, k, r]
                     )
-            for r in rs:
-                for k in range(2):
+            for k in range(2):
+                for r in rs:
                     receive(s, k, r)
                     ahead = wave[s, k, r + 1] if r < rc - 1 else from_next[s, k]
                     behind = wave[s, k, r - 1] if r > 0 else from_prev[s, k]
@@ -281,7 +312,8 @@
         step(n, False)
         return carry
 
-    lax.fori_loop(0, steps - 1, body, 0)
+    step(0, False, True)
+    lax.fori_loop(1, steps - 1, body, 0)
     slot = (steps - 1) % 2
     for k in range(2):
         dest, remote = back_old(slot, k)
@@ -294,8 +326,15 @@
         def _():
             prev_out[pl.ds(flip * rc, rc)] = wave[slot, k]
     step(steps - 1, True)
-    for which in range(3):
+    for which in (0, 2):
         give_sent(which)
+    for part in range(2):
+        for r in range(rc):
+            dest, _, _, remote = give_prev(part, r)
+
+            @pl.when(dest != ka)
+            def _():
+                remote.wait_send()
     for k in range(2):
         dest, remote = back_old(slot, k)
 
@@ -387,7 +426,7 @@
             pltpu.VMEM((2, 2) + point, jnp.float32),
             pltpu.VMEM((2, 2) + point, jnp.float32),
             sem((2, 2, rc)), sem((2, 2, rc)), sem((2, 2, 2)), sem((2, 2, 2)),
-            sem((3, 2)), sem((3, 2)), sem((2,)), sem((2,)), sem((2, rc)), sem((2, rc)),
+            sem((3, 2)), sem((3, 2)), sem((2, rc)), sem((2, rc)), sem((2,)), sem((2,)), sem((2, rc)), sem((2, rc)),
         ],
         compiler_params=pltpu.CompilerParams(
             collective_id=0, has_side_effects=True, vmem_limit_bytes=40 * 1024 * 1024

time: 93.5 us -> 90 us (0.963); the launches traced: 91.7 us -> 89.8 us
  Pallas kernels: 82.6 us -> 80.7 us
    pallas_call x1, Pallas kernels: 82.6 us -> 80.7 us  [on_device(): pl.pallas_call(functools.partial(kernel, nka, nrad, steps, rc), out_shape...]
where the time goes in v3:
time: 90 us; the launch traced here: 89.8 us
  Pallas kernels  80.7 us (90%)
  local copies, waits for them, and re-layouts  6.06 us (7%)
  between operations  1.61 us (2%)
  other arithmetic  1.35 us (2%)
    pallas_call x1, Pallas kernels, on_device(): pl.pallas_call(functools.partial(kernel, nka, nrad, steps, rc), out_shape...  80.7 us
    unnamed x14, local copies, waits for them, and re-layouts  5.65 us

profile of v3, /device:TPU:1, one launch (start us, length us, event | category | flops | bytes accessed | tf_op | source)
XLA Modules:
  0.0 89.8 jit_solution(9868413710469609320)
XLA Ops:
  0.6 0.0 copy-start
  1.5 0.1 sqrt_multiply_fusion
  1.6 0.0 copy-start.4
  1.6 0.1 broadcast_add_fusion
  1.7 0.6 copy-done.4
  2.3 0.1 constant_dynamic-slice_fusion
  2.4 0.1 broadcast_multiply_fusion.1
  2.4 0.1 reduce-precision_convert_fusion
  2.5 0.0 copy-start.5
  2.6 0.6 copy-done.5
  3.2 0.1 broadcast_multiply_fusion
  3.3 0.1 broadcast_in_dim.13.below_ref
  3.4 0.1 broadcast_in_dim.12.here_ref
  3.5 0.7 copy-done.3
  4.2 0.1 bitcast_multiply_fusion.2
  4.3 0.1 constant_dynamic-slice_fusion.1
  4.4 0.1 fusion.2
  4.7 0.3 add_multiply_fusion.diag_ref
  4.9 0.8 copy-done.1
  5.7 0.2 copy-done.2
  6.0 0.4 fusion
  6.3 80.7 %shard_map.86 = (f32[8,192,128]{2,1,0:T(8,128)S(1)}, f32[8,192,128]{2,1,0:T(8,128)S(1)}) custom-call(f32[8,192,128]{2,1,0:T(8,128)S(1)} %get-tuple-element.19.cur_ref, f32[8,192,128]{2,1,0:T(8,128)S(1)} %get-tuple-element.18.prev_ref, f32[200,192]{1,0:T(8,128)S(1)} %concatenate.15.leg_ref, bf16[256,256]{1,0:T(8,128)(2,1)S(1)} %maximum_maximum_fusion.table_ref, ...), custom_call_target="tpu_custom_call" | custom-call | tf_op jit(solution)/shard_map/pallas_call | solution.py:412
  87.1 1.3 %copy.12 = f32[1,192,8,128]{3,2,1,0:T(8,128)} copy(f32[1,192,8,128]{3,1,2,0:T(8,128)S(1)} %bitcast.42) | data formatting | bytes 1572864
  88.4 1.3 %copy.13 = f32[1,192,8,128]{3,2,1,0:T(8,128)} copy(f32[1,192,8,128]{3,1,2,0:T(8,128)S(1)} %bitcast.41) | data formatting | bytes 1572864
  (18 shorter events, 0.2 us)
Async XLA Ops:
  0.6 3.7 %copy-start = (f32[192,8,128]{2,1,0:T(8,128)S(1)}, f32[192,8,128]{2,1,0:T(8,128)}, u32[]{:S(2)}) copy-start(f32[192,8,128]{2,1,0:T(8,128)} %param.10) | copy-start | bytes 2359300
  1.6 0.7 copy-start.4
  2.5 0.7 copy-start.5
  3.3 0.9 %copy-start.3 = (f32[1,192,192]{2,1,0:T(8,128)S(1)}, f32[1,192,192]{2,1,0:T(8,128)}, u32[]{:S(2)}) copy-start(f32[1,192,192]{2,1,0:T(8,128)} %param.9) | copy-start | bytes 442372
  4.6 1.1 %copy-start.1 = (f32[1,192,8,128]{3,2,1,0:T(8,128)S(1)}, f32[1,192,8,128]{3,2,1,0:T(8,128)}, u32[]{:S(2)}) copy-start(f32[1,192,8,128]{3,2,1,0:T(8,128)} %param.7) | copy-start | bytes 2359300
  4.6 1.4 %copy-start.2 = (f32[1,192,8,128]{3,2,1,0:T(8,128)S(1)}, f32[1,192,8,128]{3,2,1,0:T(8,128)}, u32[]{:S(2)}) copy-start(f32[1,192,8,128]{3,2,1,0:T(8,128)} %param.8) | copy-start | bytes 2359300

commit v4 on v3

--- a/solution.py
+++ b/solution.py
@@ -47,7 +47,7 @@
     prev_out, cur_out,
     wave, legs, la_ref, lb_ref, shi_ref, slo_ref,
     from_lo, from_hi, from_prev, from_next,
-    k_send, k_recv, r_send, r_recv, in_send, in_recv, old_in_send, old_in_recv, old_send, old_recv, new_send, new_recv,
+    k_send, k_recv, r_send, r_recv, in_send, in_recv, old_in_send, old_in_recv, edge_send, old_send, old_recv, new_send, new_recv,
 ):
     ka, rad = lax.axis_index("ka"), lax.axis_index("rad")
     m = ka % 4
@@ -93,17 +93,23 @@
             found.append("next")
         return found + ["lo" if k == 0 else "hi"]
 
-    def send(slot, k, r):
+    def wanted(side, first, mine):
+        if not first or side in ("lo", "hi"):
+            return has[side]
+        inside = (flip == 1) if side == "prev" else (flip == 0)
+        return jnp.logical_and(has[side], jnp.logical_not(jnp.logical_and(inside, mine)))
+
+    def send(slot, k, r, first=False):
         for side in sides_of(k, r):
-            @pl.when(has[side])
+            @pl.when(wanted(side, first, y != c))
             def _():
                 copy(side, slot, k, r).start()
 
     opposite = {"lo": "hi", "hi": "lo", "prev": "next", "next": "prev"}
 
-    def receive(slot, k, r):
+    def receive(slot, k, r, first=False):
         for side in sides_of(k, r):
-            @pl.when(has[side])
+            @pl.when(wanted(side, first, jnp.logical_and(y == c, k == c)))
             def _():
                 copy(opposite[side], slot, k, r).wait_recv()
 
@@ -137,6 +143,19 @@
         )
         return dest, source, target, remote
 
+    def edge(into, row, at):
+        return pltpu.make_async_remote_copy(
+            src_ref=cur_ref.at[row], dst_ref=into.at[0, c],
+            send_sem=edge_send, recv_sem=r_recv.at[0, at, c],
+            device_id=(base + 3 * y, rad), device_id_type=MESH,
+        )
+
+    def edges(act):
+        for value, into, row, at in ((1, from_prev, rc - 1, 1), (0, from_next, rc, 0)):
+            @pl.when(jnp.logical_and(flip == value, y != c))
+            def _():
+                act(edge(into, row, at))
+
     def take_prev(k, r):
         @pl.when(base + 2 * c + k != ka)
         def _():
@@ -214,12 +233,17 @@
     pl.semaphore_wait(barrier, 3 + sum(has[side].astype(jnp.int32) for side in dev))
 
     give_start(0)
+    edges(lambda remote: remote.start())
+    for value, into, row in ((1, from_prev, rc - 1), (0, from_next, rc)):
+        @pl.when(jnp.logical_and(flip == value, y == c))
+        def _():
+            into[0, c] = cur_ref[row]
     give_start(2)
     take(0)
     for rs in order:
         for k in range(2):
             for r in rs:
-                send(0, k, r)
+                send(0, k, r, True)
     for rs in order:
         for r in rs:
             for part in range(2):
@@ -278,7 +302,7 @@
                     )
             for k in range(2):
                 for r in rs:
-                    receive(s, k, r)
+                    receive(s, k, r, first)
                     ahead = wave[s, k, r + 1] if r < rc - 1 else from_next[s, k]
                     behind = wave[s, k, r - 1] if r > 0 else from_prev[s, k]
                     upper = wave[s, 1, r] if k == 0 else from_hi[s, r]
@@ -304,7 +328,7 @@
             for r in rs:
                 for k in range(2):
                     for side in sides_of(k, r):
-                        @pl.when(has[side])
+                        @pl.when(wanted(side, first, y != c))
                         def _():
                             copy(side, s, k, r).wait_send()
 
@@ -326,6 +350,7 @@
         def _():
             prev_out[pl.ds(flip * rc, rc)] = wave[slot, k]
     step(steps - 1, True)
+    edges(lambda remote: remote.wait_send())
     for which in (0, 2):
         give_sent(which)
     for part in range(2):
@@ -426,7 +451,7 @@
             pltpu.VMEM((2, 2) + point, jnp.float32),
             pltpu.VMEM((2, 2) + point, jnp.float32),
             sem((2, 2, rc)), sem((2, 2, rc)), sem((2, 2, 2)), sem((2, 2, 2)),
-            sem((3, 2)), sem((3, 2)), sem((2, rc)), sem((2, rc)), sem((2,)), sem((2,)), sem((2, rc)), sem((2, rc)),
+            sem((3, 2)), sem((3, 2)), sem((2, rc)), sem((2, rc)), sem, sem((2,)), sem((2,)), sem((2, rc)), sem((2, rc)),
         ],
         compiler_params=pltpu.CompilerParams(
             collective_id=0, has_side_effects=True, vmem_limit_bytes=40 * 1024 * 1024

time: 90 us -> 88.1 us (0.979)
  Pallas kernels: 80.7 us -> 78.8 us
    pallas_call x1, Pallas kernels: 80.7 us -> 78.8 us  [on_device(): pl.pallas_call(functools.partial(kernel, nka, nrad, steps, rc), out_shape...]
where the time goes in v4:
time: 88.1 us; the launch traced here: 87.8 us
  Pallas kernels  78.8 us (89%)
  local copies, waits for them, and re-layouts  6.06 us (7%)
  between operations  1.61 us (2%)
  other arithmetic  1.35 us (2%)
    pallas_call x1, Pallas kernels, on_device(): pl.pallas_call(functools.partial(kernel, nka, nrad, steps, rc), out_shape...  78.8 us
    unnamed x14, local copies, waits for them, and re-layouts  5.65 us

profile of v4, /device:TPU:1, one launch (start us, length us, event | category | flops | bytes accessed | tf_op | source)
XLA Modules:
  0.0 87.8 jit_solution(10329115575617907920)
XLA Ops:
  0.6 0.0 copy-start
  1.5 0.1 sqrt_multiply_fusion
  1.6 0.1 broadcast_add_fusion
  1.7 0.6 copy-done.4
  2.3 0.1 constant_dynamic-slice_fusion
  2.4 0.1 broadcast_multiply_fusion.1
  2.4 0.1 reduce-precision_convert_fusion
  2.5 0.0 copy-start.5
  2.6 0.6 copy-done.5
  3.2 0.1 broadcast_multiply_fusion
  3.3 0.1 broadcast_in_dim.13.below_ref
  3.4 0.1 broadcast_in_dim.12.here_ref
  3.5 0.7 copy-done.3
  4.2 0.1 bitcast_multiply_fusion.2
  4.3 0.1 constant_dynamic-slice_fusion.1
  4.4 0.1 fusion.2
  4.6 0.0 copy-start.1
  4.7 0.3 add_multiply_fusion.diag_ref
  4.9 0.8 copy-done.1
  5.7 0.2 copy-done.2
  6.0 0.4 fusion
  6.3 78.8 %shard_map.86 = (f32[8,192,128]{2,1,0:T(8,128)S(1)}, f32[8,192,128]{2,1,0:T(8,128)S(1)}) custom-call(f32[8,192,128]{2,1,0:T(8,128)S(1)} %get-tuple-element.19.cur_ref, f32[8,192,128]{2,1,0:T(8,128)S(1)} %get-tuple-element.18.prev_ref, f32[200,192]{1,0:T(8,128)S(1)} %concatenate.15.leg_ref, bf16[256,256]{1,0:T(8,128)(2,1)S(1)} %maximum_maximum_fusion.table_ref, ...), custom_call_target="tpu_custom_call" | custom-call | tf_op jit(solution)/shard_map/pallas_call | solution.py:437
  85.2 1.3 %copy.12 = f32[1,192,8,128]{3,2,1,0:T(8,128)} copy(f32[1,192,8,128]{3,1,2,0:T(8,128)S(1)} %bitcast.42) | data formatting | bytes 1572864
  86.5 1.3 %copy.13 = f32[1,192,8,128]{3,2,1,0:T(8,128)} copy(f32[1,192,8,128]{3,1,2,0:T(8,128)S(1)} %bitcast.41) | data formatting | bytes 1572864
  (18 shorter events, 0.2 us)
Async XLA Ops:
  0.6 3.7 %copy-start = (f32[192,8,128]{2,1,0:T(8,128)S(1)}, f32[192,8,128]{2,1,0:T(8,128)}, u32[]{:S(2)}) copy-start(f32[192,8,128]{2,1,0:T(8,128)} %param.10) | copy-start | bytes 2359300
  1.6 0.7 copy-start.4
  2.5 0.7 copy-start.5
  3.3 0.9 %copy-start.3 = (f32[1,192,192]{2,1,0:T(8,128)S(1)}, f32[1,192,192]{2,1,0:T(8,128)}, u32[]{:S(2)}) copy-start(f32[1,192,192]{2,1,0:T(8,128)} %param.9) | copy-start | bytes 442372
  4.6 1.1 %copy-start.1 = (f32[1,192,8,128]{3,2,1,0:T(8,128)S(1)}, f32[1,192,8,128]{3,2,1,0:T(8,128)}, u32[]{:S(2)}) copy-start(f32[1,192,8,128]{3,2,1,0:T(8,128)} %param.7) | copy-start | bytes 2359300
  4.6 1.4 %copy-start.2 = (f32[1,192,8,128]{3,2,1,0:T(8,128)S(1)}, f32[1,192,8,128]{3,2,1,0:T(8,128)}, u32[]{:S(2)}) copy-start(f32[1,192,8,128]{3,2,1,0:T(8,128)} %param.8) | copy-start | bytes 2359300
